TPU v7x, 512 devices: a whole 4x4x16 slice. The times are simulated.
512 devices in a mesh: slab: 8 (over y_lo, x), tile: 64 (over z, y_hi, core).
Axes of the slice: x: 4, y: 4 (y_hi: 2, y_lo: 2; y = y_hi * 2 + y_lo), z: 16, core: 2. Of those that a mesh axis runs over, the one named last changes fastest.
Arguments:
- phase: float32 [8, 4096, 2048], P('slab', 'tile'), may hold values from -3.140625 to 3.140625
- absorption: float32 [8, 4096, 2048], P('slab', 'tile'), may hold values from 0.02 to 0.5
- probe: bfloat16 [2, 512, 512], replicated, may hold values from -3 to 3
- taps: bfloat16 [2, 65], replicated, as said below
- offsets: int32 [2, 16], replicated, may hold values from 0 to 1536, as said below
- intensity: float32 [2, 512, 8, 2, 512], P(None, 'tile'), may hold values from 0.05 to 4
Outputs:
- object_grad: float32 [8, 2, 4096, 2048], P('slab', None, 'tile')
Inputs may be any that keep to these rules, and one draw needn't show every extreme that they name: offsets[b, g * 2 + q] is the first object column of the window of position q of row band g in batch b. `taps`: tap m acts at offset m - 32.
All inputs are finite; a program needn't handle non-finite values.
Results may differ from a plain program's by a relative error of at most 0.04.
Values may be sent and summed in bfloat16 or wider, within the bound.
A program may use at most 64 MiB of HBM per device.

v0:
```python
import math

import jax
import jax.numpy as jnp
from jax import lax
from jax.sharding import PartitionSpec as P

WIN = 512
HALF = 32
POS_BAND = 2
BATCHES = 2


def padded_2(value, sides, width):
    for axis, dim in sides:
        devices, length = (lax.axis_size(axis), value.shape[dim])
        up = [(i, (i + 1) % devices) for i in range(devices)]
        down = [(j, i) for i, j in up]
        last = lax.slice_in_dim(value, length - width, length, axis=dim)
        first = lax.slice_in_dim(value, 0, width, axis=dim)
        before = lax.ppermute(last, axis, up)
        after = lax.ppermute(first, axis, down)
        value = jnp.concatenate([before, value, after], axis=dim)
    return value


def shifted(value, axis, steps):
    count = lax.axis_size(axis)
    first, last = (max(0, -steps), min(count, count - steps))
    return lax.ppermute(value, axis, [(source, source + steps) for source in range(first, last)])


def toeplitz(vector, row_count, col_count):
    width = vector.shape[0]
    padded = jnp.concatenate([vector, jnp.zeros((col_count - width + 1,), vector.dtype)])
    flat = jnp.tile(padded, row_count)[: row_count * col_count]
    return flat.reshape(row_count, col_count)


def fourier_tables(length):
    index_line = jnp.arange(length, dtype=jnp.int32)
    product_mod = index_line[:, None] * index_line[None, :] % length
    angles = product_mod.astype(jnp.float32) * (2.0 * math.pi / length)
    return (jnp.cos(angles).astype(jnp.bfloat16), jnp.sin(angles).astype(jnp.bfloat16))


def complex_rows(matrix_re, matrix_im, field):

    def product(matrix, values):
        return jnp.einsum("ij,pjx->pix", matrix, values, preferred_element_type=jnp.float32)

    field_re = field[:, 0]
    field_im = field[:, 1]
    out_re = product(matrix_re, field_re) - product(matrix_im, field_im)
    out_im = product(matrix_re, field_im) + product(matrix_im, field_re)
    return jnp.stack([out_re, out_im], axis=1)


def complex_cols(matrix_re, matrix_im, field):

    def product(matrix, values):
        return jnp.einsum("pij,cj->pic", values, matrix, preferred_element_type=jnp.float32)

    field_re = field[:, 0]
    field_im = field[:, 1]
    out_re = product(matrix_re, field_re) - product(matrix_im, field_im)
    out_im = product(matrix_re, field_im) + product(matrix_im, field_re)
    return jnp.stack([out_re, out_im], axis=1)


def device_roll(field, count, amount):
    shape = field.shape
    split = field.reshape(shape[:3] + (count, shape[3] // count))
    return jnp.roll(split, amount, axis=3).reshape(shape)


def on_device(phase, absorption, probe, taps, offsets, intensity):
    strip_rows = phase.shape[1]
    per_band = WIN // strip_rows
    half_band = per_band // 2
    band_count = intensity.shape[2]
    tile_pos = lax.axis_index("tile")
    tile_count = lax.axis_size("tile")
    slab_pos = lax.axis_index("slab")
    slab_count = lax.axis_size("slab")
    shifted_pos = (tile_pos - half_band) % tile_count
    band_index = shifted_pos // per_band
    within = shifted_pos % per_band
    split_count = 1
    group_size = POS_BAND // split_count
    micro_count = BATCHES * split_count
    is_last = slab_pos == slab_count - 1
    decay = jnp.exp(-absorption[0])
    trans_re = decay * jnp.cos(phase[0])
    trans_im = decay * jnp.sin(phase[0])
    trans_pair = jnp.stack([trans_re, trans_im])
    taps_re = taps[0].astype(jnp.float32)
    taps_im = taps[1].astype(jnp.float32)
    adj_re = taps_re[::-1]
    adj_im = -taps_im[::-1]
    wide_rows = strip_rows + 2 * HALF
    fore_row_re = toeplitz(taps_re, strip_rows, wide_rows).astype(jnp.bfloat16)
    fore_row_im = toeplitz(taps_im, strip_rows, wide_rows).astype(jnp.bfloat16)
    back_row_re = toeplitz(adj_re, strip_rows, wide_rows).astype(jnp.bfloat16)
    back_row_im = toeplitz(adj_im, strip_rows, wide_rows).astype(jnp.bfloat16)
    fore_col_re = toeplitz(taps_re, WIN, WIN + 2 * HALF)[:, HALF : HALF + WIN].astype(jnp.bfloat16)
    fore_col_im = toeplitz(taps_im, WIN, WIN + 2 * HALF)[:, HALF : HALF + WIN].astype(jnp.bfloat16)
    back_col_re = toeplitz(adj_re, WIN, WIN + 2 * HALF)[:, HALF : HALF + WIN].astype(jnp.bfloat16)
    back_col_im = toeplitz(adj_im, WIN, WIN + 2 * HALF)[:, HALF : HALF + WIN].astype(jnp.bfloat16)
    halo_lines = jnp.arange(wide_rows)
    lower_cut = (halo_lines < HALF) & (within == 0)
    upper_cut = (halo_lines >= strip_rows + HALF) & (within == per_band - 1)
    rim_keep = jnp.where(lower_cut | upper_cut, 0.0, 1.0).astype(jnp.bfloat16)[:, None]

    def extend(field):
        return padded_2(field, (("tile", 2),), HALF) * rim_keep

    band_offsets = lax.dynamic_slice_in_dim(offsets, band_index * POS_BAND, POS_BAND, 1)

    def windows(col_starts):
        return jax.vmap(lambda col_at: lax.dynamic_slice_in_dim(trans_pair, col_at, WIN, 2))(
            col_starts
        )

    probe_rows = lax.dynamic_slice_in_dim(probe, within * strip_rows, strip_rows, 1)
    entry = jnp.broadcast_to(probe_rows[None], (group_size, 2, strip_rows, WIN))

    def forward_slice(incoming, col_starts, active):
        window = windows(col_starts)
        values = incoming.astype(jnp.float32)
        lit_re = values[:, 0] * window[:, 0] - values[:, 1] * window[:, 1]
        lit_im = values[:, 0] * window[:, 1] + values[:, 1] * window[:, 0]
        lit = jnp.stack([lit_re, lit_im], axis=1).astype(jnp.bfloat16)
        spread = complex_rows(fore_row_re, fore_row_im, extend(lit)).astype(jnp.bfloat16)
        return lax.cond(
            active,
            lambda field: complex_cols(fore_col_re, fore_col_im, field).astype(jnp.bfloat16),
            lambda field: jnp.zeros_like(field),
            spread,
        )

    zero_wave = jnp.zeros((group_size, 2, strip_rows, WIN), jnp.bfloat16)
    empty_store = jnp.zeros((micro_count, group_size, 2, strip_rows, WIN), jnp.bfloat16)

    def forward_step(section_index, carry):
        current, saved, exits = carry
        arrived = shifted(current, "slab", 1)
        batch_index = section_index - slab_pos
        active = (batch_index >= 0) & (batch_index < micro_count)
        slot_index = jnp.clip(batch_index, 0, micro_count - 1)
        start = jnp.where(slab_pos == 0, entry, arrived)
        result = forward_slice(start, band_offsets[slot_index], active)
        previous = lax.dynamic_index_in_dim(saved, slot_index, 0, keepdims=False)
        saved = lax.dynamic_update_index_in_dim(
            saved, jnp.where(active, start, previous), slot_index, 0
        )
        earlier = lax.dynamic_index_in_dim(exits, slot_index, 0, keepdims=False)
        exits = lax.dynamic_update_index_in_dim(
            exits, jnp.where(active & is_last, result, earlier), slot_index, 0
        )
        return (result, saved, exits)

    current, saved, exits = lax.fori_loop(
        0, micro_count + slab_count - 1, forward_step, (zero_wave, empty_store, empty_store)
    )
    cos_table, sin_table = fourier_tables(WIN)
    norm_scale = WIN ** (-0.5)
    flat_width = POS_BAND * strip_rows

    def column_transform(field):

        def product(values, matrix):
            return jnp.einsum("bprx,kx->bkpr", values, matrix, preferred_element_type=jnp.float32)

        exit_re = field[:, :, 0]
        exit_im = field[:, :, 1]
        spec_re = (product(exit_re, cos_table) + product(exit_im, sin_table)) * norm_scale
        spec_im = (product(exit_im, cos_table) - product(exit_re, sin_table)) * norm_scale
        stacked = jnp.stack([spec_re, spec_im], axis=1)
        return stacked.reshape(BATCHES, 2, WIN, flat_width).astype(jnp.bfloat16)

    spectra = lax.cond(
        is_last,
        column_transform,
        lambda field: jnp.zeros((BATCHES, 2, WIN, flat_width), jnp.bfloat16),
        exits,
    )
    arrived_cols = lax.all_to_all(spectra, "tile", split_axis=2, concat_axis=3, tiled=True)
    arrived_cols = device_roll(arrived_cols, tile_count, -half_band)
    cos_rows = cos_table.reshape(WIN, per_band, strip_rows)
    sin_rows = sin_table.reshape(WIN, per_band, strip_rows)

    def detector(field):
        freq_count = field.shape[2]
        pieces = field.reshape(BATCHES, 2, freq_count, band_count, per_band, POS_BAND, strip_rows)

        def forward_product(matrix, values):
            return jnp.einsum(
                "ysr,bkgspr->bkgpy", matrix, values, preferred_element_type=jnp.float32
            )

        def adjoint_product(matrix, values):
            return jnp.einsum(
                "ysr,bkgpy->bkgspr", matrix, values, preferred_element_type=jnp.float32
            )

        far_re = (
            forward_product(cos_rows, pieces[:, 0]) + forward_product(sin_rows, pieces[:, 1])
        ) * norm_scale
        far_im = (
            forward_product(cos_rows, pieces[:, 1]) - forward_product(sin_rows, pieces[:, 0])
        ) * norm_scale
        excess = far_re * far_re + far_im * far_im - intensity
        err_re = (excess * far_re).astype(jnp.bfloat16)
        err_im = (excess * far_im).astype(jnp.bfloat16)
        spec_back_re = (
            adjoint_product(cos_rows, err_re) - adjoint_product(sin_rows, err_im)
        ) * norm_scale
        spec_back_im = (
            adjoint_product(cos_rows, err_im) + adjoint_product(sin_rows, err_re)
        ) * norm_scale
        stacked = jnp.stack([spec_back_re, spec_back_im], axis=1)
        return stacked.reshape(BATCHES, 2, freq_count, band_count * per_band * flat_width).astype(
            jnp.bfloat16
        )

    errors = lax.cond(is_last, detector, lambda field: jnp.zeros_like(field), arrived_cols)
    errors = device_roll(errors, tile_count, half_band)
    returned = lax.all_to_all(errors, "tile", split_axis=3, concat_axis=2, tiled=True)

    def column_adjoint(field):
        pieces = field.reshape(BATCHES, 2, WIN, POS_BAND, strip_rows)

        def product(values, matrix):
            return jnp.einsum("bkpr,kx->bprx", values, matrix, preferred_element_type=jnp.float32)

        grad_re = (product(pieces[:, 0], cos_table) - product(pieces[:, 1], sin_table)) * norm_scale
        grad_im = (product(pieces[:, 1], cos_table) + product(pieces[:, 0], sin_table)) * norm_scale
        stacked = jnp.stack([grad_re, grad_im], axis=2).astype(jnp.bfloat16)
        return stacked

    feedback = lax.cond(is_last, column_adjoint, lambda field: empty_store, returned)

    def backward_slice(incoming, kept, col_starts, active, grads):
        spread = lax.cond(
            active,
            lambda field: complex_cols(back_col_re, back_col_im, field).astype(jnp.bfloat16),
            lambda field: jnp.zeros_like(field),
            incoming,
        )
        local_grad = complex_rows(back_row_re, back_row_im, extend(spread))
        seen = kept.astype(jnp.float32)
        window = windows(col_starts)
        inc_re = local_grad[:, 0] * seen[:, 0] + local_grad[:, 1] * seen[:, 1]
        inc_im = local_grad[:, 1] * seen[:, 0] - local_grad[:, 0] * seen[:, 1]
        increments = jnp.stack([inc_re, inc_im], axis=1) * active.astype(jnp.float32)

        def place(member, running):
            current_cols = lax.dynamic_slice(
                running, (0, 0, col_starts[member]), (2, strip_rows, WIN)
            )
            return lax.dynamic_update_slice(
                running, current_cols + increments[member], (0, 0, col_starts[member])
            )

        grads = lax.fori_loop(0, group_size, place, grads)
        out_re = window[:, 0] * local_grad[:, 0] + window[:, 1] * local_grad[:, 1]
        out_im = window[:, 0] * local_grad[:, 1] - window[:, 1] * local_grad[:, 0]
        return (jnp.stack([out_re, out_im], axis=1).astype(jnp.bfloat16), grads)

    def backward_step(section_index, carry):
        current, grads = carry
        arrived = shifted(current, "slab", -1)
        batch_index = section_index - (slab_count - 1 - slab_pos)
        active = (batch_index >= 0) & (batch_index < micro_count)
        slot_index = jnp.clip(batch_index, 0, micro_count - 1)
        start = jnp.where(is_last, feedback[slot_index], arrived)
        return backward_slice(start, saved[slot_index], band_offsets[slot_index], active, grads)

    grad_start = jnp.zeros((2, strip_rows, phase.shape[2]), jnp.float32)
    current, grads = lax.fori_loop(
        0, micro_count + slab_count - 1, backward_step, (zero_wave, grad_start)
    )
    phase_grad = grads[1] * trans_re - grads[0] * trans_im
    absorb_grad = -(grads[0] * trans_re + grads[1] * trans_im)
    return jnp.stack([phase_grad, absorb_grad])[None]


def solution(mesh):
    placed = (
        P("slab", "tile", None),
        P("slab", "tile", None),
        P(),
        P(),
        P(),
        P(None, "tile", None, None, None),
    )
    return jax.shard_map(
        on_device,
        mesh=mesh,
        in_specs=placed,
        out_specs=P("slab", None, "tile", None),
        check_vma=False,
    )
```

profile of v0, /device:TPU:6, one launch (start us, length us, event | category | flops | bytes accessed | tf_op | source)
XLA Modules:
  0.0 782.7 jit_solution(10859255704462255816)
XLA Ops:
  20.5 270.2 %while.65 = (s32[]{:T(128)}, bf16[2,2,64,512]{3,2,0,1:T(8,128)(2,1)}, bf16[2,2,2,64,512]{4,3,1,2,0:T(8,128)(2,1)}, bf16[2,2,2,64,512]{4,3,1,2,0:T(8,128)(2,1)}, ...) while((s32[]{:T(128)}, ...), condition=%wide.region_3.4_spmd.clone, body=%wide.region_0.3_spmd.clone.sunk | while | flops 340657024 | bytes 23922200 | solution.py:163
  30.8 12.6 %collective-permute-start.1 = (bf16[2,2,32,512]{3,2,0,1:T(8,128)(2,1)S(1)}, bf16[2,2,32,512]{3,2,0,1:T(8,128)(2,1)S(1)}, u32[]{:S(2)}, u32[]{:S(2)}) collective-permute-start(bf16[2,2,32,512]{3,2,0,1:T(8,128)(2,1)S(1)} %get-tuple-element.1456), channel_id=1, source_target_pairs={{1,0},{2,1},{3,2},{4,3},{5,4},{6,5},{7,6},{8,7},{9,8},{10,9},{11,1... | collective-permute-start | bytes 393224 | tf_op jit(solution)/shard_map/while/body/eval_jaxpr/ppermute | solution.py:22
  46.7 6.8 collective-permute-done.2
  76.0 6.3 collective-permute-done.2
  104.5 6.3 collective-permute-done.2
  161.4 6.3 collective-permute-done.2
  292.4 10.0 %all-to-all-start = ((bf16[2,2,512,128]{3,1,0,2:T(2,128)(2,1)}), bf16[2,2,512,128]{3,1,0,2:T(2,128)(2,1)S(1)}, u32[]{:S(2)}, u32[]{:S(2)}) async-start(bf16[2,2,512,128]{3,1,0,2:T(2,128)(2,1)} %copy.74), calls=%async_computation | async-start | bytes 1048576 | tf_op jit(solution)/shard_map/all_to_all | solution.py:188
  307.2 28.8 %all-to-all-done = bf16[2,2,512,128]{3,1,0,2:T(2,128)(2,1)S(1)} async-done(((bf16[2,2,512,128]{3,1,0,2:T(2,128)(2,1)}), bf16[2,2,512,128]{3,1,0,2:T(2,128)(2,1)S(1)}, u32[]{:S(2)}, u32[]{:S(2)}) %all-to-all-start) | async-done | bytes 524320 | tf_op jit(solution)/shard_map/all_to_all | solution.py:188
  336.7 9.4 %copy.79 = bf16[2,2,8,64,128]{2,1,0,4,3:T(2,128)(2,1)} copy(bf16[2,2,8,64,128]{4,3,2,0,1:T(8,128)(2,1)S(1)} %pad_maximum_fusion.10) | data formatting | bytes 1048576 | tf_op jit(solution)/shard_map/jit(_roll_static)/concatenate | solution.py:74
  346.0 11.2 %reshape.212 = bf16[64,2,2048]{2,1,0:T(2,128)(2,1)} reshape(bf16[8192,2,2,8]{3,2,1,0:T(2,128)(2,1)} %bitcast.446) | data formatting | bytes 1048576
  368.3 28.1 %all-to-all-done.1 = bf16[64,2,2048]{2,1,0:T(2,128)(2,1)S(1)} async-done(((bf16[64,2,2048]{2,1,0:T(2,128)(2,1)}), bf16[64,2,2048]{2,1,0:T(2,128)(2,1)S(1)}, u32[]{:S(2)}, u32[]{:S(2)}) %all-to-all-start.1) | async-done | bytes 524320 | tf_op jit(solution)/shard_map/all_to_all | solution.py:229
  396.3 10.9 %reshape.213 = bf16[8192,2,2,8]{3,2,1,0:T(2,128)(2,1)} reshape(bf16[64,2,2048]{2,1,0:T(2,128)(2,1)S(1)} %all-to-all-done.1) | data formatting | bytes 1048576
  407.3 11.7 %copy.107 = bf16[2,2,8,64,128]{4,3,2,1,0:T(8,128)(2,1)S(1)} copy(bf16[2,2,8,64,128]{2,1,0,4,3:T(2,128)(2,1)} %bitcast.447) | data formatting | bytes 1048576 | tf_op jit(solution)/shard_map/all_to_all | solution.py:229
  420.9 359.1 %while.67 = (s32[]{:T(128)}, bf16[2,2,64,512]{3,2,0,1:T(8,128)(2,1)}, f32[2,64,2048]{2,1,0:T(8,128)S(1)}, s32[]{:T(128)}, s32[2,2]{1,0:T(2,128)}, /*index=5*/f32...) while((s32[]{:T(128)}, ...), condition=%wide.region_15.16_spmd.clone, body=%wide.region_10.15_spmd.clone.sunk | while | flops 339805056 | bytes 25036140 | solution.py:281
  450.3 8.7 %while.68 = (s32[]{:T(128)}, f32[2,64,2048]{2,1,0:T(8,128)S(1)}, s32[2]{0:T(128)}, f32[2,2,64,512]{3,2,0,1:T(8,128)S(1)}, s32[]{:T(128)}, /*index=5*/s32[]{:T(128)}, s32[]{:T(128)}) while((s32[]{:T(128)}, f32[2,64,2048]{2,1,0:T(8,128)S(1)}, s32[2]{0:T(128)}, f32[2,2,64,512]{3,2,0,1:T(8,128)S(1)}, s32[]{:T(128)}, /*index=5*/s32[]{:T(128)}, ...), condition=%wide.region_14.14_spmd, body=%wide.region_13.13_spmd.sunk | while | flops 65541 | bytes 1310855 | solution.py:266
  488.8 8.7 %while.68 = (s32[]{:T(128)}, f32[2,64,2048]{2,1,0:T(8,128)S(1)}, s32[2]{0:T(128)}, f32[2,2,64,512]{3,2,0,1:T(8,128)S(1)}, s32[]{:T(128)}, /*index=5*/s32[]{:T(128)}, s32[]{:T(128)}) while((s32[]{:T(128)}, f32[2,64,2048]{2,1,0:T(8,128)S(1)}, s32[2]{0:T(128)}, f32[2,2,64,512]{3,2,0,1:T(8,128)S(1)}, s32[]{:T(128)}, /*index=5*/s32[]{:T(128)}, ...), condition=%wide.region_14.14_spmd, body=%wide.region_13.13_spmd.sunk | while | flops 65541 | bytes 1310855 | solution.py:266
  527.2 8.7 %while.68 = (s32[]{:T(128)}, f32[2,64,2048]{2,1,0:T(8,128)S(1)}, s32[2]{0:T(128)}, f32[2,2,64,512]{3,2,0,1:T(8,128)S(1)}, s32[]{:T(128)}, /*index=5*/s32[]{:T(128)}, s32[]{:T(128)}) while((s32[]{:T(128)}, f32[2,64,2048]{2,1,0:T(8,128)S(1)}, s32[2]{0:T(128)}, f32[2,2,64,512]{3,2,0,1:T(8,128)S(1)}, s32[]{:T(128)}, /*index=5*/s32[]{:T(128)}, ...), condition=%wide.region_14.14_spmd, body=%wide.region_13.13_spmd.sunk | while | flops 65541 | bytes 1310855 | solution.py:266
  545.5 6.5 collective-permute-done.3
  571.3 8.7 %while.68 = (s32[]{:T(128)}, f32[2,64,2048]{2,1,0:T(8,128)S(1)}, s32[2]{0:T(128)}, f32[2,2,64,512]{3,2,0,1:T(8,128)S(1)}, s32[]{:T(128)}, /*index=5*/s32[]{:T(128)}, s32[]{:T(128)}) while((s32[]{:T(128)}, f32[2,64,2048]{2,1,0:T(8,128)S(1)}, s32[2]{0:T(128)}, f32[2,2,64,512]{3,2,0,1:T(8,128)S(1)}, s32[]{:T(128)}, /*index=5*/s32[]{:T(128)}, ...), condition=%wide.region_14.14_spmd, body=%wide.region_13.13_spmd.sunk | while | flops 65541 | bytes 1310855 | solution.py:266
  616.5 8.7 %while.68 = (s32[]{:T(128)}, f32[2,64,2048]{2,1,0:T(8,128)S(1)}, s32[2]{0:T(128)}, f32[2,2,64,512]{3,2,0,1:T(8,128)S(1)}, s32[]{:T(128)}, /*index=5*/s32[]{:T(128)}, s32[]{:T(128)}) while((s32[]{:T(128)}, f32[2,64,2048]{2,1,0:T(8,128)S(1)}, s32[2]{0:T(128)}, f32[2,2,64,512]{3,2,0,1:T(8,128)S(1)}, s32[]{:T(128)}, /*index=5*/s32[]{:T(128)}, ...), condition=%wide.region_14.14_spmd, body=%wide.region_13.13_spmd.sunk | while | flops 65541 | bytes 1310855 | solution.py:266
  658.2 8.0 %while.68 = (s32[]{:T(128)}, f32[2,64,2048]{2,1,0:T(8,128)S(1)}, s32[2]{0:T(128)}, f32[2,2,64,512]{3,2,0,1:T(8,128)S(1)}, s32[]{:T(128)}, /*index=5*/s32[]{:T(128)}, s32[]{:T(128)}) while((s32[]{:T(128)}, f32[2,64,2048]{2,1,0:T(8,128)S(1)}, s32[2]{0:T(128)}, f32[2,2,64,512]{3,2,0,1:T(8,128)S(1)}, s32[]{:T(128)}, /*index=5*/s32[]{:T(128)}, ...), condition=%wide.region_14.14_spmd, body=%wide.region_13.13_spmd.sunk | while | flops 65541 | bytes 1310855 | solution.py:266
  696.3 8.0 %while.68 = (s32[]{:T(128)}, f32[2,64,2048]{2,1,0:T(8,128)S(1)}, s32[2]{0:T(128)}, f32[2,2,64,512]{3,2,0,1:T(8,128)S(1)}, s32[]{:T(128)}, /*index=5*/s32[]{:T(128)}, s32[]{:T(128)}) while((s32[]{:T(128)}, f32[2,64,2048]{2,1,0:T(8,128)S(1)}, s32[2]{0:T(128)}, f32[2,2,64,512]{3,2,0,1:T(8,128)S(1)}, s32[]{:T(128)}, /*index=5*/s32[]{:T(128)}, ...), condition=%wide.region_14.14_spmd, body=%wide.region_13.13_spmd.sunk | while | flops 65541 | bytes 1310855 | solution.py:266
  733.8 8.0 %while.68 = (s32[]{:T(128)}, f32[2,64,2048]{2,1,0:T(8,128)S(1)}, s32[2]{0:T(128)}, f32[2,2,64,512]{3,2,0,1:T(8,128)S(1)}, s32[]{:T(128)}, /*index=5*/s32[]{:T(128)}, s32[]{:T(128)}) while((s32[]{:T(128)}, f32[2,64,2048]{2,1,0:T(8,128)S(1)}, s32[2]{0:T(128)}, f32[2,2,64,512]{3,2,0,1:T(8,128)S(1)}, s32[]{:T(128)}, /*index=5*/s32[]{:T(128)}, ...), condition=%wide.region_14.14_spmd, body=%wide.region_13.13_spmd.sunk | while | flops 65541 | bytes 1310855 | solution.py:266
  771.2 8.0 %while.68 = (s32[]{:T(128)}, f32[2,64,2048]{2,1,0:T(8,128)S(1)}, s32[2]{0:T(128)}, f32[2,2,64,512]{3,2,0,1:T(8,128)S(1)}, s32[]{:T(128)}, /*index=5*/s32[]{:T(128)}, s32[]{:T(128)}) while((s32[]{:T(128)}, f32[2,64,2048]{2,1,0:T(8,128)S(1)}, s32[2]{0:T(128)}, f32[2,2,64,512]{3,2,0,1:T(8,128)S(1)}, s32[]{:T(128)}, /*index=5*/s32[]{:T(128)}, ...), condition=%wide.region_14.14_spmd, body=%wide.region_13.13_spmd.sunk | while | flops 65541 | bytes 1310855 | solution.py:266
  (773 shorter events, 604.2 us)
Async XLA Ops:
  20.5 10.1 %collective-permute-start = (bf16[2,2,64,512]{3,2,0,1:T(8,128)(2,1)}, bf16[2,2,64,512]{3,2,0,1:T(8,128)(2,1)S(1)}, u32[]{:S(2)}, u32[]{:S(2)}) collective-permute-start(bf16[2,2,64,512]{3,2,0,1:T(8,128)(2,1)} %get-tuple-element.1530), channel_id=1, source_target_pairs={{0,64},{64,128},{128,192},{192,256},{256,320},{320,384},{384,448},... | collective-permute-start | bytes 786440 | tf_op jit(solution)/shard_map/while/body/eval_jaxpr/ppermute | solution.py:30
  30.8 15.1 %collective-permute-start.1 = (bf16[2,2,32,512]{3,2,0,1:T(8,128)(2,1)S(1)}, bf16[2,2,32,512]{3,2,0,1:T(8,128)(2,1)S(1)}, u32[]{:S(2)}, u32[]{:S(2)}) collective-permute-start(bf16[2,2,32,512]{3,2,0,1:T(8,128)(2,1)S(1)} %get-tuple-element.1456), channel_id=1, source_target_pairs={{1,0},{2,1},{3,2},{4,3},{5,4},{6,5},{7,6},{8,7},{9,8},{10,9},{11,1... | collective-permute-start | bytes 393224 | tf_op jit(solution)/shard_map/while/body/eval_jaxpr/ppermute | solution.py:22
  43.4 10.0 %collective-permute-start.2 = (bf16[2,2,32,512]{3,2,0,1:T(8,128)(2,1)S(1)}, bf16[2,2,32,512]{3,2,0,1:T(8,128)(2,1)}, u32[]{:S(2)}, u32[]{:S(2)}) collective-permute-start(bf16[2,2,32,512]{3,2,0,1:T(8,128)(2,1)S(1)} %get-tuple-element.1457), channel_id=1, source_target_pairs={{0,1},{1,2},{2,3},{3,4},{4,5},{5,6},{6,7},{7,8},{8,9},{9,10},{10,1... | collective-permute-start | bytes 393224 | tf_op jit(solution)/shard_map/while/body/eval_jaxpr/ppermute | solution.py:21
  59.2 11.0 %collective-permute-start = (bf16[2,2,64,512]{3,2,0,1:T(8,128)(2,1)}, bf16[2,2,64,512]{3,2,0,1:T(8,128)(2,1)S(1)}, u32[]{:S(2)}, u32[]{:S(2)}) collective-permute-start(bf16[2,2,64,512]{3,2,0,1:T(8,128)(2,1)} %get-tuple-element.1530), channel_id=1, source_target_pairs={{0,64},{64,128},{128,192},{192,256},{256,320},{320,384},{384,448},... | collective-permute-start | bytes 786440 | tf_op jit(solution)/shard_map/while/body/eval_jaxpr/ppermute | solution.py:30
  72.4 10.0 %collective-permute-start.2 = (bf16[2,2,32,512]{3,2,0,1:T(8,128)(2,1)S(1)}, bf16[2,2,32,512]{3,2,0,1:T(8,128)(2,1)}, u32[]{:S(2)}, u32[]{:S(2)}) collective-permute-start(bf16[2,2,32,512]{3,2,0,1:T(8,128)(2,1)S(1)} %get-tuple-element.1457), channel_id=1, source_target_pairs={{0,1},{1,2},{2,3},{3,4},{4,5},{5,6},{6,7},{7,8},{8,9},{9,10},{10,1... | collective-permute-start | bytes 393224 | tf_op jit(solution)/shard_map/while/body/eval_jaxpr/ppermute | solution.py:21
  88.1 10.6 %collective-permute-start = (bf16[2,2,64,512]{3,2,0,1:T(8,128)(2,1)}, bf16[2,2,64,512]{3,2,0,1:T(8,128)(2,1)S(1)}, u32[]{:S(2)}, u32[]{:S(2)}) collective-permute-start(bf16[2,2,64,512]{3,2,0,1:T(8,128)(2,1)} %get-tuple-element.1530), channel_id=1, source_target_pairs={{0,64},{64,128},{128,192},{192,256},{256,320},{320,384},{384,448},... | collective-permute-start | bytes 786440 | tf_op jit(solution)/shard_map/while/body/eval_jaxpr/ppermute | solution.py:30
  100.8 10.0 %collective-permute-start.2 = (bf16[2,2,32,512]{3,2,0,1:T(8,128)(2,1)S(1)}, bf16[2,2,32,512]{3,2,0,1:T(8,128)(2,1)}, u32[]{:S(2)}, u32[]{:S(2)}) collective-permute-start(bf16[2,2,32,512]{3,2,0,1:T(8,128)(2,1)S(1)} %get-tuple-element.1457), channel_id=1, source_target_pairs={{0,1},{1,2},{2,3},{3,4},{4,5},{5,6},{6,7},{7,8},{8,9},{9,10},{10,1... | collective-permute-start | bytes 393224 | tf_op jit(solution)/shard_map/while/body/eval_jaxpr/ppermute | solution.py:21
  116.6 10.6 %collective-permute-start = (bf16[2,2,64,512]{3,2,0,1:T(8,128)(2,1)}, bf16[2,2,64,512]{3,2,0,1:T(8,128)(2,1)S(1)}, u32[]{:S(2)}, u32[]{:S(2)}) collective-permute-start(bf16[2,2,64,512]{3,2,0,1:T(8,128)(2,1)} %get-tuple-element.1530), channel_id=1, source_target_pairs={{0,64},{64,128},{128,192},{192,256},{256,320},{320,384},{384,448},... | collective-permute-start | bytes 786440 | tf_op jit(solution)/shard_map/while/body/eval_jaxpr/ppermute | solution.py:30
  157.8 10.0 %collective-permute-start.2 = (bf16[2,2,32,512]{3,2,0,1:T(8,128)(2,1)S(1)}, bf16[2,2,32,512]{3,2,0,1:T(8,128)(2,1)}, u32[]{:S(2)}, u32[]{:S(2)}) collective-permute-start(bf16[2,2,32,512]{3,2,0,1:T(8,128)(2,1)S(1)} %get-tuple-element.1457), channel_id=1, source_target_pairs={{0,1},{1,2},{2,3},{3,4},{4,5},{5,6},{6,7},{7,8},{8,9},{9,10},{10,1... | collective-permute-start | bytes 393224 | tf_op jit(solution)/shard_map/while/body/eval_jaxpr/ppermute | solution.py:21
  174.8 10.7 %collective-permute-start = (bf16[2,2,64,512]{3,2,0,1:T(8,128)(2,1)}, bf16[2,2,64,512]{3,2,0,1:T(8,128)(2,1)S(1)}, u32[]{:S(2)}, u32[]{:S(2)}) collective-permute-start(bf16[2,2,64,512]{3,2,0,1:T(8,128)(2,1)} %get-tuple-element.1530), channel_id=1, source_target_pairs={{0,64},{64,128},{128,192},{192,256},{256,320},{320,384},{384,448},... | collective-permute-start | bytes 786440 | tf_op jit(solution)/shard_map/while/body/eval_jaxpr/ppermute | solution.py:30
  203.4 11.8 %collective-permute-start = (bf16[2,2,64,512]{3,2,0,1:T(8,128)(2,1)}, bf16[2,2,64,512]{3,2,0,1:T(8,128)(2,1)S(1)}, u32[]{:S(2)}, u32[]{:S(2)}) collective-permute-start(bf16[2,2,64,512]{3,2,0,1:T(8,128)(2,1)} %get-tuple-element.1530), channel_id=1, source_target_pairs={{0,64},{64,128},{128,192},{192,256},{256,320},{320,384},{384,448},... | collective-permute-start | bytes 786440 | tf_op jit(solution)/shard_map/while/body/eval_jaxpr/ppermute | solution.py:30
  233.1 11.0 %collective-permute-start = (bf16[2,2,64,512]{3,2,0,1:T(8,128)(2,1)}, bf16[2,2,64,512]{3,2,0,1:T(8,128)(2,1)S(1)}, u32[]{:S(2)}, u32[]{:S(2)}) collective-permute-start(bf16[2,2,64,512]{3,2,0,1:T(8,128)(2,1)} %get-tuple-element.1530), channel_id=1, source_target_pairs={{0,64},{64,128},{128,192},{192,256},{256,320},{320,384},{384,448},... | collective-permute-start | bytes 786440 | tf_op jit(solution)/shard_map/while/body/eval_jaxpr/ppermute | solution.py:30
  262.0 10.8 %collective-permute-start = (bf16[2,2,64,512]{3,2,0,1:T(8,128)(2,1)}, bf16[2,2,64,512]{3,2,0,1:T(8,128)(2,1)S(1)}, u32[]{:S(2)}, u32[]{:S(2)}) collective-permute-start(bf16[2,2,64,512]{3,2,0,1:T(8,128)(2,1)} %get-tuple-element.1530), channel_id=1, source_target_pairs={{0,64},{64,128},{128,192},{192,256},{256,320},{320,384},{384,448},... | collective-permute-start | bytes 786440 | tf_op jit(solution)/shard_map/while/body/eval_jaxpr/ppermute | solution.py:30
  292.4 43.7 %all-to-all-start = ((bf16[2,2,512,128]{3,1,0,2:T(2,128)(2,1)}), bf16[2,2,512,128]{3,1,0,2:T(2,128)(2,1)S(1)}, u32[]{:S(2)}, u32[]{:S(2)}) async-start(bf16[2,2,512,128]{3,1,0,2:T(2,128)(2,1)} %copy.74), calls=%async_computation | async-start | bytes 1048576 | tf_op jit(solution)/shard_map/all_to_all | solution.py:188
  357.2 39.1 %all-to-all-start.1 = ((bf16[64,2,2048]{2,1,0:T(2,128)(2,1)}), bf16[64,2,2048]{2,1,0:T(2,128)(2,1)S(1)}, u32[]{:S(2)}, u32[]{:S(2)}) async-start(bf16[64,2,2048]{2,1,0:T(2,128)(2,1)} %reshape.212), calls=%async_computation.1 | async-start | bytes 1048576 | tf_op jit(solution)/shard_map/all_to_all | solution.py:229
  420.9 12.8 %collective-permute-start.3 = (bf16[2,2,64,512]{3,2,0,1:T(8,128)(2,1)}, bf16[2,2,64,512]{3,2,0,1:T(8,128)(2,1)S(1)}, u32[]{:S(2)}, u32[]{:S(2)}) collective-permute-start(bf16[2,2,64,512]{3,2,0,1:T(8,128)(2,1)} %get-tuple-element.1591), channel_id=1, source_target_pairs={{64,0},{128,64},{192,128},{256,192},{320,256},{384,320},{448,384},... | collective-permute-start | bytes 786440 | tf_op jit(solution)/shard_map/while/body/eval_jaxpr/ppermute | solution.py:30
  459.8 10.6 %collective-permute-start.3 = (bf16[2,2,64,512]{3,2,0,1:T(8,128)(2,1)}, bf16[2,2,64,512]{3,2,0,1:T(8,128)(2,1)S(1)}, u32[]{:S(2)}, u32[]{:S(2)}) collective-permute-start(bf16[2,2,64,512]{3,2,0,1:T(8,128)(2,1)} %get-tuple-element.1591), channel_id=1, source_target_pairs={{64,0},{128,64},{192,128},{256,192},{320,256},{384,320},{448,384},... | collective-permute-start | bytes 786440 | tf_op jit(solution)/shard_map/while/body/eval_jaxpr/ppermute | solution.py:30
  498.2 10.6 %collective-permute-start.3 = (bf16[2,2,64,512]{3,2,0,1:T(8,128)(2,1)}, bf16[2,2,64,512]{3,2,0,1:T(8,128)(2,1)S(1)}, u32[]{:S(2)}, u32[]{:S(2)}) collective-permute-start(bf16[2,2,64,512]{3,2,0,1:T(8,128)(2,1)} %get-tuple-element.1591), channel_id=1, source_target_pairs={{64,0},{128,64},{192,128},{256,192},{320,256},{384,320},{448,384},... | collective-permute-start | bytes 786440 | tf_op jit(solution)/shard_map/while/body/eval_jaxpr/ppermute | solution.py:30
  536.6 15.4 %collective-permute-start.3 = (bf16[2,2,64,512]{3,2,0,1:T(8,128)(2,1)}, bf16[2,2,64,512]{3,2,0,1:T(8,128)(2,1)S(1)}, u32[]{:S(2)}, u32[]{:S(2)}) collective-permute-start(bf16[2,2,64,512]{3,2,0,1:T(8,128)(2,1)} %get-tuple-element.1591), channel_id=1, source_target_pairs={{64,0},{128,64},{192,128},{256,192},{320,256},{384,320},{448,384},... | collective-permute-start | bytes 786440 | tf_op jit(solution)/shard_map/while/body/eval_jaxpr/ppermute | solution.py:30
  580.7 14.2 %collective-permute-start.3 = (bf16[2,2,64,512]{3,2,0,1:T(8,128)(2,1)}, bf16[2,2,64,512]{3,2,0,1:T(8,128)(2,1)S(1)}, u32[]{:S(2)}, u32[]{:S(2)}) collective-permute-start(bf16[2,2,64,512]{3,2,0,1:T(8,128)(2,1)} %get-tuple-element.1591), channel_id=1, source_target_pairs={{64,0},{128,64},{192,128},{256,192},{320,256},{384,320},{448,384},... | collective-permute-start | bytes 786440 | tf_op jit(solution)/shard_map/while/body/eval_jaxpr/ppermute | solution.py:30
  626.0 12.0 %collective-permute-start.3 = (bf16[2,2,64,512]{3,2,0,1:T(8,128)(2,1)}, bf16[2,2,64,512]{3,2,0,1:T(8,128)(2,1)S(1)}, u32[]{:S(2)}, u32[]{:S(2)}) collective-permute-start(bf16[2,2,64,512]{3,2,0,1:T(8,128)(2,1)} %get-tuple-element.1591), channel_id=1, source_target_pairs={{64,0},{128,64},{192,128},{256,192},{320,256},{384,320},{448,384},... | collective-permute-start | bytes 786440 | tf_op jit(solution)/shard_map/while/body/eval_jaxpr/ppermute | solution.py:30
  667.0 10.7 %collective-permute-start.3 = (bf16[2,2,64,512]{3,2,0,1:T(8,128)(2,1)}, bf16[2,2,64,512]{3,2,0,1:T(8,128)(2,1)S(1)}, u32[]{:S(2)}, u32[]{:S(2)}) collective-permute-start(bf16[2,2,64,512]{3,2,0,1:T(8,128)(2,1)} %get-tuple-element.1591), channel_id=1, source_target_pairs={{64,0},{128,64},{192,128},{256,192},{320,256},{384,320},{448,384},... | collective-permute-start | bytes 786440 | tf_op jit(solution)/shard_map/while/body/eval_jaxpr/ppermute | solution.py:30
  705.1 10.7 %collective-permute-start.3 = (bf16[2,2,64,512]{3,2,0,1:T(8,128)(2,1)}, bf16[2,2,64,512]{3,2,0,1:T(8,128)(2,1)S(1)}, u32[]{:S(2)}, u32[]{:S(2)}) collective-permute-start(bf16[2,2,64,512]{3,2,0,1:T(8,128)(2,1)} %get-tuple-element.1591), channel_id=1, source_target_pairs={{64,0},{128,64},{192,128},{256,192},{320,256},{384,320},{448,384},... | collective-permute-start | bytes 786440 | tf_op jit(solution)/shard_map/while/body/eval_jaxpr/ppermute | solution.py:30
  742.5 10.7 %collective-permute-start.3 = (bf16[2,2,64,512]{3,2,0,1:T(8,128)(2,1)}, bf16[2,2,64,512]{3,2,0,1:T(8,128)(2,1)S(1)}, u32[]{:S(2)}, u32[]{:S(2)}) collective-permute-start(bf16[2,2,64,512]{3,2,0,1:T(8,128)(2,1)} %get-tuple-element.1591), channel_id=1, source_target_pairs={{64,0},{128,64},{192,128},{256,192},{320,256},{384,320},{448,384},... | collective-permute-start | bytes 786440 | tf_op jit(solution)/shard_map/while/body/eval_jaxpr/ppermute | solution.py:30
  (125 other events, 813.7 us)
where the time goes:
time: 797 us; the launch traced here: 783 us
  local copies, waits for them, and re-layouts  252 us (32%)
  waiting for transfers between devices  189 us (24%)
  starting transfers between devices  169 us (21%)
  other arithmetic  90.4 us (11%)
  matrix products  43.1 us (5%)
  loops' own time  38.7 us (5%)
    ppermute x18, waiting for transfers between devices, padded_2(): before = lax.ppermute(last, axis, up)  104 us
    ppermute x18, starting transfers between devices, padded_2(): after = lax.ppermute(first, axis, down)  59.4 us
    gather x18, local copies, waits for them, and re-layouts, windows(): lax.dynamic_slice_in_dim(trans_pair, col_at, WIN, 2)  58.7 us
    ppermute x18, starting transfers between devices, shifted(): lax.ppermute(value, axis, [(source, source + steps) for source in range(f...  55.4 us
    ppermute x18, starting transfers between devices, padded_2(): before = lax.ppermute(last, axis, up)  39 us
    dot_general x72, matrix products, product(): jnp.einsum('ij,pjx->pix', matrix, values, preferred_element_type=jnp.floa...  38.2 us
    while x198, local copies, waits for them, and re-layouts  36.7 us
    another operation x9, loops' own time, backward_slice(): grads = lax.fori_loop(0, group_size, place, grads)  34.8 us
  transfers between devices with their start and end apart: 56, of which 30 were waited for; matrix products, arithmetic and copies ran while one was open for 20% of the time, Pallas kernels for 0%

commit v1 on v0

v1 whole, which is shorter than its diff:
```python
import functools
import math

import jax
import jax.numpy as jnp
import numpy as np
from jax import lax
from jax.experimental import pallas as pl
from jax.experimental.pallas import tpu as pltpu
from jax.sharding import PartitionSpec as P

MESH = pl.DeviceIdType.MESH
F32 = jnp.float32
BF16 = jnp.bfloat16
WIN = 512
HALF = 32
NXO = 2048
SLICES = 8
STRIP = 64
ROWS = 128
SCALE = WIN**-0.5


def dot(a, b):
    return jnp.dot(a, b, preferred_element_type=F32)


def fourier_tables():
    line = np.arange(WIN)
    angles = (line[:, None] * line[None, :] % WIN).astype(np.float64) * (2.0 * math.pi / WIN)
    return np.cos(angles).astype(np.float32), np.sin(angles).astype(np.float32)


def sincos(x):
    h = 0.5 * x
    q = h * h
    s = -2.50521084e-8
    for term in (2.75573192e-6, -1.98412698e-4, 8.33333333e-3, -1.66666667e-1, 1.0):
        s = s * q + term
    s = s * h
    c = 2.08767570e-9
    for term in (-2.75573192e-7, 2.48015873e-5, -1.38888889e-3, 4.16666667e-2, -0.5, 1.0):
        c = c * q + term
    return 2.0 * s * c, 1.0 - 2.0 * s * s


def prepare_kernel(info, phase, absorb, intensity, win, trans, ints, wide):
    for part in range(4):
        rows = pl.ds(part * 16, 16)
        sin_part, cos_part = sincos(phase[rows, :])
        decay = jnp.exp(-absorb[rows, :])
        real, imag = decay * cos_part, decay * sin_part
        trans[0, rows, :] = real
        trans[1, rows, :] = imag
        wide[0, rows, :NXO] = real
        wide[1, rows, :NXO] = imag
    wide[:, :, NXO:] = jnp.zeros((2, STRIP, 128), F32)
    for p in range(4):
        start = info[p]
        base = pl.multiple_of(start // 128 * 128, 128)
        turn = (640 - start % 128) % 640
        for part in range(2):
            block = wide[part, :, pl.ds(base, 640)]
            win[p, part] = pltpu.roll(block, turn, 1)[:, :WIN].astype(BF16)
        ints[p] = intensity[p // 2, :, 0, p % 2, :]


def prepare(info, phase, absorb, intensity):
    vmem = pl.BlockSpec(memory_space=pltpu.VMEM)
    return pl.pallas_call(
        prepare_kernel,
        grid_spec=pltpu.PrefetchScalarGridSpec(
            num_scalar_prefetch=1,
            grid=(1,),
            in_specs=[
                pl.BlockSpec((STRIP, NXO), lambda i, info: (0, 0)),
                pl.BlockSpec((STRIP, NXO), lambda i, info: (0, 0)),
                pl.BlockSpec((2, 8, 1, 2, WIN), lambda i, info: (0, 0, info[4], 0, 0)),
            ],
            out_specs=[
                pl.BlockSpec((4, 2, STRIP, WIN), lambda i, info: (0, 0, 0, 0)),
                pl.BlockSpec((2, STRIP, NXO), lambda i, info: (0, 0, 0)),
                pl.BlockSpec((4, 8, WIN), lambda i, info: (0, 0, 0)),
            ],
            scratch_shapes=[pltpu.VMEM((2, STRIP, NXO + 128), F32)],
        ),
        out_shape=[
            jax.ShapeDtypeStruct((4, 2, STRIP, WIN), BF16),
            jax.ShapeDtypeStruct((2, STRIP, NXO), F32),
            jax.ShapeDtypeStruct((4, 8, WIN), F32),
        ],
        compiler_params=pltpu.CompilerParams(vmem_limit_bytes=32 << 20),
        name="prepare",
    )(info, phase, absorb, intensity)


def finish_kernel(info, inc, trans, out, wide):
    wide[...] = jnp.zeros_like(wide)
    blank = jnp.zeros((STRIP, 128), F32)
    for p in range(4):
        start = info[p]
        base = pl.multiple_of(start // 128 * 128, 128)
        for part in range(2):
            block = jnp.concatenate([inc[p, part].astype(F32), blank], axis=1)
            wide[part, :, pl.ds(base, 640)] += pltpu.roll(block, start % 128, 1)
    real, imag = trans[0], trans[1]
    grad_re, grad_im = wide[0, :, :NXO], wide[1, :, :NXO]
    out[0] = grad_im * real - grad_re * imag
    out[1] = -(grad_re * real + grad_im * imag)


def finish(info, inc, trans):
    vmem = pl.BlockSpec(memory_space=pltpu.VMEM)
    return pl.pallas_call(
        finish_kernel,
        in_specs=[pl.BlockSpec(memory_space=pltpu.SMEM), vmem, vmem],
        out_specs=vmem,
        out_shape=jax.ShapeDtypeStruct((2, STRIP, NXO), F32),
        scratch_shapes=[pltpu.VMEM((2, STRIP, NXO + 128), F32)],
        compiler_params=pltpu.CompilerParams(vmem_limit_bytes=32 << 20),
        name="finish",
    )(info, inc, trans)


def device_at(x, y, z, core):
    return ((y % 2) * 4 + x, (z % 16) * 4 + (y // 2) * 2 + core)


def member_at(band, p, c):
    upper = c // 2
    return device_at(p, 0 * p, 2 * band + 1 + upper, (c + upper) % 2)


def strip_at(band, layer, w):
    return (layer, (band * 8 + 4 + w) % 64)


def same(a, b):
    return (a[0] == b[0]) & (a[1] == b[1])


def chain_kernel(
    win, ints, probe, line, cos_hbm, sin_hbm, out,
    trans, waves, lits, gmids, incs, halo, acc, gwave,
    row_own, row_halo, col_w, cos_t, sin_t, int_in, int_t,
    stage, spec_in, back_out, back_in,
    win_send, win_recv, int_send, int_recv, halo_send, halo_recv,
    inc_send, inc_recv, spec_send, spec_recv, back_send, back_recv, table_sem,
):
    slab = lax.axis_index("slab")
    tile = lax.axis_index("tile")
    me = (slab, tile)
    band = ((tile + 60) % 64) // 8
    w = (tile + 60) % 8
    x, y = slab % 4, (tile // 2) % 2 * 2 + slab // 4
    upper = w // 4
    is_member = y == 0
    p_me = x
    c_me = upper * 2 + (tile % 2 + upper) % 2

    def signal(device):
        pl.semaphore_signal(pltpu.get_barrier_semaphore(), 1, device_id=device, device_id_type=MESH)

    @pl.when(is_member)
    def _():
        def greet(i, _):
            signal(strip_at(band, i // 2, 2 * c_me + i % 2))
            signal((band, 16 * c_me + i))
            return 0

        lax.fori_loop(0, 16, greet, 0)
        for d in range(1, 4):
            signal(member_at(band, p_me, (c_me + d) % 4))

    for p in range(4):
        signal(member_at(band, jnp.int32(p), w // 2))
    barrier = pltpu.get_barrier_semaphore()

    @pl.when(is_member)
    def _():
        pl.semaphore_wait(barrier, 16 + 3 + 8)

    @pl.when(jnp.logical_not(is_member))
    def _():
        pl.semaphore_wait(barrier, 8)

    half = pl.ds(pl.multiple_of((w % 2) * STRIP, STRIP), STRIP)
    for p in range(4):
        target = member_at(band, jnp.int32(p), w // 2)

        @pl.when(same(target, me))
        def _():
            pltpu.make_async_copy(
                win.at[p], trans.at[slab, :, half, :], win_recv.at[slab, w % 2]
            ).start()

        @pl.when(jnp.logical_not(same(target, me)))
        def _():
            pltpu.make_async_remote_copy(
                src_ref=win.at[p],
                dst_ref=trans.at[slab, :, half, :],
                send_sem=win_send.at[p],
                recv_sem=win_recv.at[slab, w % 2],
                device_id=target,
                device_id_type=MESH,
            ).start()

    for p in range(4):
        target = member_at(slab, jnp.int32(p), tile // 16)

        @pl.when(same(target, me))
        def _():
            pltpu.make_async_copy(
                ints.at[p], int_in.at[tile % 16], int_recv.at[tile % 16]
            ).start()

        @pl.when(jnp.logical_not(same(target, me)))
        def _():
            pltpu.make_async_remote_copy(
                src_ref=ints.at[p],
                dst_ref=int_in.at[tile % 16],
                send_sem=int_send.at[p],
                recv_sem=int_recv.at[tile % 16],
                device_id=target,
                device_id_type=MESH,
            ).start()

    def toeplitz(row, shift):
        lanes = jnp.broadcast_to(line[row : row + 1, :], (128, 256))
        return pltpu.roll(lanes, shift, 1, stride=1, stride_axis=0)

    def build(direction):
        plain, turned = (0, 2) if direction == 0 else (2, 0)
        sign = 1.0 if direction == 0 else -1.0
        real = toeplitz(plain, 224)
        imag = sign * toeplitz(plain + 1, 224)
        row_own[direction, :128, :128] = real[:, :128].astype(BF16)
        row_own[direction, :128, 128:] = (-imag[:, :128]).astype(BF16)
        row_own[direction, 128:, :128] = imag[:, :128].astype(BF16)
        row_own[direction, 128:, 128:] = real[:, :128].astype(BF16)
        rim_re, rim_im = real[:, 128:], imag[:, 128:]
        lane = lax.broadcasted_iota(jnp.int32, (128, 128), 1)

        def weave(first, second):
            low = jnp.where(lane < 32, first, pltpu.roll(first, 64, 1))
            high = jnp.where(lane < 96, pltpu.roll(second, 64, 1), second)
            return jnp.where(lane < 64, low, high)

        row_halo[direction, :128, :] = weave(rim_re, -rim_im).astype(BF16)
        row_halo[direction, 128:, :] = weave(rim_im, rim_re).astype(BF16)
        for part in range(2):
            factor = 1.0 if part == 0 else sign
            far_part = factor * toeplitz(turned + part, 96)[:, :128]
            near_part = factor * toeplitz(turned + part, 224)[:, :128]
            columns = pl.ds(part * 128, 128)
            col_w[direction, :128, columns] = jnp.where(lane < 32, far_part, 0.0).astype(BF16)
            col_w[direction, 128:256, columns] = near_part.astype(BF16)
            col_w[direction, 256:, columns] = jnp.where(lane >= 96, far_part, 0.0).astype(BF16)

    def along_columns(field, direction):
        reals, imags = [], []
        for j in range(4):
            low, high = max(0, j - 1), min(4, j + 2)
            weights = col_w[direction, (low - j + 1) * 128 : (high - j + 1) * 128, :]
            both = dot(field[:, low * 128 : high * 128], weights)
            reals.append(both[:128, :128] - both[128:, 128:])
            imags.append(both[:128, 128:] + both[128:, :128])
        return jnp.concatenate(reals, axis=1), jnp.concatenate(imags, axis=1)

    def halo_copies(step, field):
        above = pltpu.make_async_remote_copy(
            src_ref=field.at[:, 0:HALF, :],
            dst_ref=halo.at[step, :, 0],
            send_sem=halo_send.at[step, 0],
            recv_sem=halo_recv.at[step, 0],
            device_id=member_at(band, p_me, (c_me + 3) % 4),
            device_id_type=MESH,
        )
        below = pltpu.make_async_remote_copy(
            src_ref=field.at[:, ROWS - HALF : ROWS, :],
            dst_ref=halo.at[step, :, 1],
            send_sem=halo_send.at[step, 1],
            recv_sem=halo_recv.at[step, 1],
            device_id=member_at(band, p_me, (c_me + 1) % 4),
            device_id_type=MESH,
        )
        return above, below

    def halo_start(step, field):
        above, below = halo_copies(step, field)

        @pl.when(c_me > 0)
        def _():
            above.start()

        @pl.when(c_me < 3)
        def _():
            below.start()

    def halo_wait(step, field, sends):
        above, below = halo_copies(step, field)

        @pl.when(c_me < 3)
        def _():
            if sends:
                below.wait_send()
            else:
                above.wait_recv()

        @pl.when(c_me > 0)
        def _():
            if sends:
                above.wait_send()
            else:
                below.wait_recv()

    def along_rows(step, field, direction):
        acc[...] = dot(row_own[direction], field[...].reshape(2 * ROWS, WIN))
        halo_wait(step, field, False)
        rim = halo[step].reshape(4 * HALF, WIN)
        return acc[...] + dot(row_halo[direction], rim)

    @pl.when(is_member)
    def _():
        tables = [
            pltpu.make_async_copy(cos_hbm, cos_t, table_sem.at[0]),
            pltpu.make_async_copy(sin_hbm, sin_t, table_sem.at[1]),
            pltpu.make_async_copy(
                probe.at[:, pl.ds(pl.multiple_of(c_me * ROWS, ROWS), ROWS), :],
                waves.at[0],
                table_sem.at[2],
            ),
        ]
        for copy in tables:
            copy.start()
        build(0)
        build(1)

        @pl.when(c_me == 0)
        def _():
            halo[:, :, 1] = jnp.zeros((16, 2, HALF, WIN), BF16)

        @pl.when(c_me == 3)
        def _():
            halo[:, :, 0] = jnp.zeros((16, 2, HALF, WIN), BF16)

        for copy in tables:
            copy.wait()

        def forward(s, _):
            for j in range(2):
                part = trans.at[s, :, pl.ds(j * STRIP, STRIP), :]
                pltpu.make_async_copy(part, part, win_recv.at[s, j]).wait()
            field = lits.at[s]

            def light(rows):
                wave_re = waves[s, 0, rows, :].astype(F32)
                wave_im = waves[s, 1, rows, :].astype(F32)
                trans_re = trans[s, 0, rows, :].astype(F32)
                trans_im = trans[s, 1, rows, :].astype(F32)
                field[0, rows, :] = (wave_re * trans_re - wave_im * trans_im).astype(BF16)
                field[1, rows, :] = (wave_re * trans_im + wave_im * trans_re).astype(BF16)

            light(pl.ds(0, HALF))
            light(pl.ds(ROWS - HALF, HALF))
            halo_start(s, field)
            light(pl.ds(HALF, ROWS - 2 * HALF))
            mid = along_rows(s, field, 0).astype(BF16)
            real, imag = along_columns(mid, 0)
            waves[s + 1, 0] = real.astype(BF16)
            waves[s + 1, 1] = imag.astype(BF16)
            return 0

        lax.fori_loop(0, SLICES, forward, 0)

        for i in range(16):
            pltpu.make_async_copy(int_in.at[i], int_in.at[i], int_recv.at[i]).wait()
        int_t[...] = int_in[...].reshape(128, WIN).T

        exit_wave = waves[SLICES].reshape(2 * ROWS, WIN)
        by_cos, by_sin = dot(exit_wave, cos_t[...]), dot(exit_wave, sin_t[...])
        spec_re = ((by_cos[:128] + by_sin[128:]) * SCALE).astype(BF16)
        spec_im = ((by_cos[128:] - by_sin[:128]) * SCALE).astype(BF16)
        for k in range(4):
            stage[k, :, :128] = spec_re[:, k * 128 : (k + 1) * 128]
            stage[k, :, 128:] = spec_im[:, k * 128 : (k + 1) * 128]

        mine = pl.ds(pl.multiple_of(c_me * ROWS, ROWS), ROWS)

        def spec_copy(d):
            other = (c_me + d) % 4
            return pltpu.make_async_remote_copy(
                src_ref=stage.at[other],
                dst_ref=spec_in.at[mine, :],
                send_sem=spec_send.at[d],
                recv_sem=spec_recv.at[d],
                device_id=member_at(band, p_me, other),
                device_id_type=MESH,
            )

        for d in range(1, 4):
            spec_copy(d).start()
        spec_in[mine, :] = stage[c_me]
        for d in range(1, 4):
            spec_copy(d).wait()

        spectrum = spec_in[...]
        by_cos, by_sin = dot(cos_t[...], spectrum), dot(sin_t[...], spectrum)
        far_re = (by_cos[:, :128] + by_sin[:, 128:]) * SCALE
        far_im = (by_cos[:, 128:] - by_sin[:, :128]) * SCALE
        excess = far_re * far_re + far_im * far_im - int_t[...]
        err = jnp.concatenate(
            [(excess * far_re).astype(BF16), (excess * far_im).astype(BF16)], axis=1
        )
        by_cos, by_sin = dot(cos_t[...], err), dot(sin_t[...], err)
        back_re = ((by_cos[:, :128] - by_sin[:, 128:]) * SCALE).astype(BF16)
        back_im = ((by_cos[:, 128:] + by_sin[:, :128]) * SCALE).astype(BF16)
        for k in range(4):
            back_out[k, :, :128] = back_re[k * 128 : (k + 1) * 128]
            back_out[k, :, 128:] = back_im[k * 128 : (k + 1) * 128]

        def back_copy(d):
            other = (c_me + d) % 4
            return pltpu.make_async_remote_copy(
                src_ref=back_out.at[other],
                dst_ref=back_in.at[c_me],
                send_sem=back_send.at[d],
                recv_sem=back_recv.at[d],
                device_id=member_at(band, p_me, other),
                device_id_type=MESH,
            )

        for d in range(1, 4):
            back_copy(d).start()
        back_in[c_me] = back_out[c_me]
        for d in range(1, 4):
            back_copy(d).wait()

        back_all = jnp.concatenate(
            [
                jnp.concatenate([back_in[k, :, :128] for k in range(4)], axis=1),
                jnp.concatenate([back_in[k, :, 128:] for k in range(4)], axis=1),
            ],
            axis=0,
        )
        by_cos, by_sin = dot(back_all, cos_t[...]), dot(back_all, sin_t[...])
        gwave[0] = ((by_cos[:128] - by_sin[128:]) * SCALE).astype(BF16)
        gwave[1] = ((by_cos[128:] + by_sin[:128]) * SCALE).astype(BF16)

        def inc_target(s, j):
            return strip_at(band, s, 2 * c_me + j)

        def inc_copy(s, j):
            return pltpu.make_async_remote_copy(
                src_ref=incs.at[s, :, pl.ds(j * STRIP, STRIP), :],
                dst_ref=out.at[p_me],
                send_sem=inc_send.at[s, j],
                recv_sem=inc_recv.at[p_me],
                device_id=inc_target(s, j),
                device_id_type=MESH,
            )

        def backward(i, _):
            s = SLICES - 1 - i
            step = SLICES + s
            field = gmids.at[s]
            real, imag = along_columns(gwave[...].reshape(2 * ROWS, WIN), 1)
            field[0] = real.astype(BF16)
            field[1] = imag.astype(BF16)
            halo_start(step, field)
            glit = along_rows(step, field, 1)
            glit_re, glit_im = glit[:128], glit[128:]
            seen_re = waves[s, 0].astype(F32)
            seen_im = waves[s, 1].astype(F32)
            incs[s, 0] = (glit_re * seen_re + glit_im * seen_im).astype(BF16)
            incs[s, 1] = (glit_im * seen_re - glit_re * seen_im).astype(BF16)
            for j in range(2):
                local = same(inc_target(s, j), me)

                @pl.when(local)
                def _():
                    pltpu.make_async_copy(
                        incs.at[s, :, pl.ds(j * STRIP, STRIP), :], out.at[p_me], inc_recv.at[p_me]
                    ).start()

                @pl.when(jnp.logical_not(local))
                def _():
                    inc_copy(s, j).start()

            trans_re = trans[s, 0].astype(F32)
            trans_im = trans[s, 1].astype(F32)
            gwave[0] = (trans_re * glit_re + trans_im * glit_im).astype(BF16)
            gwave[1] = (trans_re * glit_im - trans_im * glit_re).astype(BF16)
            return 0

        lax.fori_loop(0, SLICES, backward, 0)

        def settle(s, _):
            halo_wait(s, lits.at[s], True)
            halo_wait(SLICES + s, gmids.at[s], True)
            for j in range(2):

                @pl.when(jnp.logical_not(same(inc_target(s, j), me)))
                def _():
                    inc_copy(s, j).wait_send()

            return 0

        lax.fori_loop(0, SLICES, settle, 0)

    for p in range(4):

        @pl.when(jnp.logical_not(same(member_at(band, jnp.int32(p), w // 2), me)))
        def _():
            pltpu.make_async_copy(win.at[p], win.at[p], win_send.at[p]).wait()

        @pl.when(jnp.logical_not(same(member_at(slab, jnp.int32(p), tile // 16), me)))
        def _():
            pltpu.make_async_copy(ints.at[p], ints.at[p], int_send.at[p]).wait()

        pltpu.make_async_copy(out.at[p], out.at[p], inc_recv.at[p]).wait()


def chain(win, ints, probe, line):
    hbm = pl.BlockSpec(memory_space=pl.ANY)
    vmem = pl.BlockSpec(memory_space=pltpu.VMEM)
    cos_table, sin_table = (jnp.asarray(t, BF16) for t in fourier_tables())
    dma = pltpu.SemaphoreType.DMA
    group = (2, ROWS, WIN)
    return pl.pallas_call(
        chain_kernel,
        in_specs=[hbm, hbm, hbm, vmem, hbm, hbm],
        out_specs=hbm,
        out_shape=jax.ShapeDtypeStruct((4, 2, STRIP, WIN), BF16),
        scratch_shapes=[
            pltpu.VMEM((SLICES,) + group, BF16),
            pltpu.VMEM((SLICES + 1,) + group, BF16),
            pltpu.VMEM((SLICES,) + group, BF16),
            pltpu.VMEM((SLICES,) + group, BF16),
            pltpu.VMEM((SLICES,) + group, BF16),
            pltpu.VMEM((2 * SLICES, 2, 2, HALF, WIN), BF16),
            pltpu.VMEM((2 * ROWS, WIN), F32),
            pltpu.VMEM(group, BF16),
            pltpu.VMEM((2, 256, 256), BF16),
            pltpu.VMEM((2, 256, 128), BF16),
            pltpu.VMEM((2, 384, 256), BF16),
            pltpu.VMEM((WIN, WIN), BF16),
            pltpu.VMEM((WIN, WIN), BF16),
            pltpu.VMEM((16, 8, WIN), F32),
            pltpu.VMEM((WIN, 128), F32),
            pltpu.VMEM((4, 128, 256), BF16),
            pltpu.VMEM((WIN, 256), BF16),
            pltpu.VMEM((4, 128, 256), BF16),
            pltpu.VMEM((4, 128, 256), BF16),
            dma((4,)),
            dma((SLICES, 2)),
            dma((4,)),
            dma((16,)),
            dma((2 * SLICES, 2)),
            dma((2 * SLICES, 2)),
            dma((SLICES, 2)),
            dma((4,)),
            dma((4,)),
            dma((4,)),
            dma((4,)),
            dma((4,)),
            dma((3,)),
        ],
        compiler_params=pltpu.CompilerParams(
            collective_id=0, has_side_effects=True, vmem_limit_bytes=48 << 20
        ),
        name="chain",
    )(win, ints, probe, line, cos_table, sin_table)


def on_device(phase, absorption, probe, taps, offsets, intensity):
    slab = lax.axis_index("slab")
    band = ((lax.axis_index("tile") + 60) % 64) // 8
    starts = lax.dynamic_slice_in_dim(offsets, band * 2, 2, 1).reshape(4)
    info = jnp.concatenate([starts, slab[None].astype(jnp.int32)])
    both = jnp.concatenate([taps, taps[:, ::-1]], axis=0).astype(F32)
    line = jnp.pad(both, ((0, 4), (0, 256 - both.shape[1])))
    win, trans, ints = prepare(info, phase[0], absorption[0], intensity)
    inc = chain(win, ints, probe, line)
    return finish(info, inc, trans)[None]


def solution(mesh):
    placed = (
        P("slab", "tile", None),
        P("slab", "tile", None),
        P(),
        P(),
        P(),
        P(None, "tile", None, None, None),
    )
    return jax.shard_map(
        on_device,
        mesh=mesh,
        in_specs=placed,
        out_specs=P("slab", None, "tile", None),
        check_vma=False,
    )
```

time: 797 us -> 123 us (0.15)
  the two profiles are of different devices: /device:TPU:6 before, /device:TPU:1 now
where the time goes in v1:
time: 123 us; the launch traced here: 122 us
  Pallas kernels  115 us (93%)
  local copies, waits for them, and re-layouts  5.74 us (5%)
    pallas_call x1, Pallas kernels, chain(): pl.pallas_call(chain_kernel, in_specs=[hbm, hbm, hbm, vmem, hbm, hbm], ou...  112 us
    unnamed x14, local copies, waits for them, and re-layouts  4.84 us

profile of v1, /device:TPU:1, one launch (start us, length us, event | category | flops | bytes accessed | tf_op | source)
XLA Modules:
  0.0 121.9 jit_solution(15113704615481541210)
XLA Ops:
  0.0 0.0 copy-start
  0.0 0.0 copy-start.1
  0.0 0.7 copy-done
  0.7 0.1 constant_dynamic-slice_fusion
  0.8 0.1 reshape.3
  0.8 0.1 pad_add_fusion.info
  0.9 0.7 rev.3
  1.7 0.7 fusion.6.line
  2.3 0.0 copy-start.4
  2.3 1.0 copy-done.4
  3.4 0.0 copy-start.5
  3.4 1.0 copy-done.5
  4.4 0.0 copy-start.6
  4.4 1.0 copy-done.6
  5.5 0.0 copy-start.2
  5.5 1.6 %prepare.1 = (bf16[4,2,64,512]{3,2,1,0:T(8,128)(2,1)S(1)}, f32[2,64,2048]{2,1,0:T(8,128)S(1)}, f32[4,8,512]{2,1,0:T(8,128)S(1)}) custom-call(s32[5]{0:T(128)S(1)} %pad_add_fusion.info, f32[64,2048]{1,0:T(8,128)S(1)} %bitcast.4, f32[64,2048]{1,0:T(8,128)S(1)} %bitcast.5, f32[2,8,8,2,512]{4,3,2,1,0:T(2,128)S(1)} %copy-done.6), custom_call_target="tpu_custom_call" | custom-call | tf_op jit(solution)/shard_map/prepare/pallas_call | solution.py:70
  7.0 0.0 copy-done.1
  7.0 0.0 copy-done.2
  7.1 0.0 copy-start.3
  7.1 1.0 copy-done.3
  8.1 111.6 %chain.1.inc = bf16[4,2,64,512]{3,2,1,0:T(8,128)(2,1)S(1)} custom-call(bf16[4,2,64,512]{3,2,1,0:T(8,128)(2,1)S(1)} %get-tuple-element.8.win, f32[4,8,512]{2,1,0:T(8,128)S(1)} %get-tuple-element.9.ints, bf16[2,512,512]{2,1,0:T(8,128)(2,1)S(1)} %copy-done.1, f32[8,256]{1,0:T(8,128)S(1)} %fusion.6.line, bf16[512,512]{1,0:T(8,128)(2,1)S(1)} %copy-done.3, ...), custom_call_target="tpu_custom_call" | custom-call | tf_op jit(solution)/shard_map/chain/pallas_call | solution.py:530
  119.7 2.2 %finish.1 = f32[2,64,2048]{2,1,0:T(8,128)} custom-call(s32[5]{0:T(128)S(1)} %pad_add_fusion.info, bf16[4,2,64,512]{3,2,1,0:T(8,128)(2,1)S(1)} %chain.1.inc, f32[2,64,2048]{2,1,0:T(8,128)S(1)} %get-tuple-element.10.trans), custom_call_target="tpu_custom_call" | custom-call | tf_op jit(solution)/shard_map/finish/pallas_call | solution.py:114
Async XLA Ops:
  0.0 0.7 copy-start
  0.0 7.0 %copy-start.1 = (bf16[2,512,512]{2,1,0:T(8,128)(2,1)S(1)}, bf16[2,512,512]{2,1,0:T(8,128)(2,1)}, u32[]{:S(2)}) copy-start(bf16[2,512,512]{2,1,0:T(8,128)(2,1)} %probe.1) | copy-start | bytes 3145732
  2.3 1.0 copy-start.4
  3.4 1.0 copy-start.5
  4.4 1.0 copy-start.6
  5.5 1.6 %copy-start.2 = (bf16[512,512]{1,0:T(8,128)(2,1)S(1)}, bf16[512,512]{1,0:T(8,128)(2,1)}, u32[]{:S(2)}) copy-start(bf16[512,512]{1,0:T(8,128)(2,1)} %constant.52.clone.sin_hbm) | copy-start | bytes 1572868
  7.1 1.0 copy-start.3

commit v2 on v1

--- a/solution.py
+++ b/solution.py
@@ -17,6 +17,7 @@
 NXO = 2048
 SLICES = 8
 STRIP = 64
+AHEAD = 4
 ROWS = 128
 SCALE = WIN**-0.5
 
@@ -44,17 +45,18 @@
     return 2.0 * s * c, 1.0 - 2.0 * s * s
 
 
+CHUNK = 16
+
+
 def prepare_kernel(info, phase, absorb, intensity, win, trans, ints, wide):
-    for part in range(4):
-        rows = pl.ds(part * 16, 16)
-        sin_part, cos_part = sincos(phase[rows, :])
-        decay = jnp.exp(-absorb[rows, :])
-        real, imag = decay * cos_part, decay * sin_part
-        trans[0, rows, :] = real
-        trans[1, rows, :] = imag
-        wide[0, rows, :NXO] = real
-        wide[1, rows, :NXO] = imag
-    wide[:, :, NXO:] = jnp.zeros((2, STRIP, 128), F32)
+    sin_part, cos_part = sincos(phase[...])
+    decay = jnp.exp(-absorb[...])
+    real, imag = decay * cos_part, decay * sin_part
+    trans[0] = real
+    trans[1] = imag
+    wide[0, :, :NXO] = real
+    wide[1, :, :NXO] = imag
+    wide[:, :, NXO:] = jnp.zeros((2, CHUNK, 128), F32)
     for p in range(4):
         start = info[p]
         base = pl.multiple_of(start // 128 * 128, 128)
@@ -62,34 +64,39 @@
         for part in range(2):
             block = wide[part, :, pl.ds(base, 640)]
             win[p, part] = pltpu.roll(block, turn, 1)[:, :WIN].astype(BF16)
-        ints[p] = intensity[p // 2, :, 0, p % 2, :]
+
+    @pl.when(pl.program_id(0) == 0)
+    def _():
+        for p in range(4):
+            values = intensity[p // 2, :, 0, p % 2, :]
+            halves = [values[:, : WIN // 2], values[:, WIN // 2 :]]
+            ints[p] = jnp.concatenate(halves, axis=0).astype(BF16)
 
 
 def prepare(info, phase, absorb, intensity):
-    vmem = pl.BlockSpec(memory_space=pltpu.VMEM)
     return pl.pallas_call(
         prepare_kernel,
         grid_spec=pltpu.PrefetchScalarGridSpec(
             num_scalar_prefetch=1,
-            grid=(1,),
+            grid=(STRIP // CHUNK,),
             in_specs=[
-                pl.BlockSpec((STRIP, NXO), lambda i, info: (0, 0)),
-                pl.BlockSpec((STRIP, NXO), lambda i, info: (0, 0)),
+                pl.BlockSpec((CHUNK, NXO), lambda i, info: (i, 0)),
+                pl.BlockSpec((CHUNK, NXO), lambda i, info: (i, 0)),
                 pl.BlockSpec((2, 8, 1, 2, WIN), lambda i, info: (0, 0, info[4], 0, 0)),
             ],
             out_specs=[
-                pl.BlockSpec((4, 2, STRIP, WIN), lambda i, info: (0, 0, 0, 0)),
-                pl.BlockSpec((2, STRIP, NXO), lambda i, info: (0, 0, 0)),
-                pl.BlockSpec((4, 8, WIN), lambda i, info: (0, 0, 0)),
+                pl.BlockSpec((4, 2, CHUNK, WIN), lambda i, info: (0, 0, i, 0)),
+                pl.BlockSpec((2, CHUNK, NXO), lambda i, info: (0, i, 0)),
+                pl.BlockSpec((4, 16, WIN // 2), lambda i, info: (0, 0, 0)),
             ],
-            scratch_shapes=[pltpu.VMEM((2, STRIP, NXO + 128), F32)],
+            scratch_shapes=[pltpu.VMEM((2, CHUNK, NXO + 128), F32)],
         ),
         out_shape=[
             jax.ShapeDtypeStruct((4, 2, STRIP, WIN), BF16),
             jax.ShapeDtypeStruct((2, STRIP, NXO), F32),
-            jax.ShapeDtypeStruct((4, 8, WIN), F32),
+            jax.ShapeDtypeStruct((4, 16, WIN // 2), BF16),
         ],
-        compiler_params=pltpu.CompilerParams(vmem_limit_bytes=32 << 20),
+        compiler_params=pltpu.CompilerParams(vmem_limit_bytes=60 << 20),
         name="prepare",
     )(info, phase, absorb, intensity)
 
@@ -128,7 +135,7 @@
 
 def member_at(band, p, c):
     upper = c // 2
-    return device_at(p, 0 * p, 2 * band + 1 + upper, (c + upper) % 2)
+    return device_at(p, p, 2 * band + 1 + upper, (c + upper) % 2)
 
 
 def strip_at(band, layer, w):
@@ -140,11 +147,11 @@
 
 
 def chain_kernel(
-    win, ints, probe, line, cos_hbm, sin_hbm, out,
-    trans, waves, lits, gmids, incs, halo, acc, gwave,
-    row_own, row_halo, col_w, cos_t, sin_t, int_in, int_t,
+    win, ints, probe, taps, cos_hbm, sin_hbm, out,
+    line, trans, waves, lits, gmids, incs, halo, acc, gwave,
+    row_rim, row_core, row_halo, col_w, cos_t, sin_t, int_in, int_t,
     stage, spec_in, back_out, back_in,
-    win_send, win_recv, int_send, int_recv, halo_send, halo_recv,
+    credit, win_send, win_recv, int_send, int_recv, halo_send, halo_recv,
     inc_send, inc_recv, spec_send, spec_recv, back_send, back_recv, table_sem,
 ):
     slab = lax.axis_index("slab")
@@ -154,7 +161,7 @@
     w = (tile + 60) % 8
     x, y = slab % 4, (tile // 2) % 2 * 2 + slab // 4
     upper = w // 4
-    is_member = y == 0
+    is_member = y == x
     p_me = x
     c_me = upper * 2 + (tile % 2 + upper) % 2
 
@@ -185,25 +192,31 @@
         pl.semaphore_wait(barrier, 8)
 
     half = pl.ds(pl.multiple_of((w % 2) * STRIP, STRIP), STRIP)
-    for p in range(4):
-        target = member_at(band, jnp.int32(p), w // 2)
-
-        @pl.when(same(target, me))
-        def _():
-            pltpu.make_async_copy(
-                win.at[p], trans.at[slab, :, half, :], win_recv.at[slab, w % 2]
-            ).start()
-
-        @pl.when(jnp.logical_not(same(target, me)))
-        def _():
-            pltpu.make_async_remote_copy(
-                src_ref=win.at[p],
-                dst_ref=trans.at[slab, :, half, :],
-                send_sem=win_send.at[p],
-                recv_sem=win_recv.at[slab, w % 2],
-                device_id=target,
-                device_id_type=MESH,
-            ).start()
+
+    def hand_out():
+        for p in range(4):
+            target = member_at(band, jnp.int32(p), w // 2)
+
+            @pl.when(same(target, me))
+            def _():
+                pltpu.make_async_copy(
+                    win.at[p], trans.at[slab, :, half, :], win_recv.at[slab, w % 2]
+                ).start()
+
+            @pl.when(jnp.logical_not(same(target, me)))
+            def _():
+                pltpu.make_async_remote_copy(
+                    src_ref=win.at[p],
+                    dst_ref=trans.at[slab, :, half, :],
+                    send_sem=win_send.at[p],
+                    recv_sem=win_recv.at[slab, w % 2],
+                    device_id=target,
+                    device_id_type=MESH,
+                ).start()
+
+    @pl.when(slab < AHEAD)
+    def _():
+        hand_out()
 
     for p in range(4):
         target = member_at(slab, jnp.int32(p), tile // 16)
@@ -225,19 +238,48 @@
                 device_id_type=MESH,
             ).start()
 
+    @pl.when((slab >= AHEAD) & jnp.logical_not(is_member))
+    def _():
+        pl.semaphore_wait(credit, 4)
+        hand_out()
+
+    def ask(s):
+        @pl.when(slab == s)
+        def _():
+            hand_out()
+
+        @pl.when((c_me % 2) * 2 + s // 4 != s % 4)
+        def _():
+            for j in range(2):
+                pl.semaphore_signal(
+                    credit,
+                    1,
+                    device_id=strip_at(band, s, 2 * c_me + j),
+                    device_id_type=MESH,
+                )
+
     def toeplitz(row, shift):
         lanes = jnp.broadcast_to(line[row : row + 1, :], (128, 256))
         return pltpu.roll(lanes, shift, 1, stride=1, stride_axis=0)
 
     def build(direction):
-        plain, turned = (0, 2) if direction == 0 else (2, 0)
+        plain, turned = (0, 8) if direction == 0 else (8, 0)
         sign = 1.0 if direction == 0 else -1.0
         real = toeplitz(plain, 224)
         imag = sign * toeplitz(plain + 1, 224)
-        row_own[direction, :128, :128] = real[:, :128].astype(BF16)
-        row_own[direction, :128, 128:] = (-imag[:, :128]).astype(BF16)
-        row_own[direction, 128:, :128] = imag[:, :128].astype(BF16)
-        row_own[direction, 128:, 128:] = real[:, :128].astype(BF16)
+        def rows(part):
+            own = part[:, :128]
+            return jnp.concatenate([own[:HALF], own[ROWS - HALF :]], axis=0), own[HALF : ROWS - HALF]
+
+        (rim_real, core_real), (rim_imag, core_imag) = rows(real), rows(imag)
+        for matrix, re_part, im_part in (
+            (row_rim, rim_real, rim_imag),
+            (row_core, core_real, core_imag),
+        ):
+            matrix[direction, :64, :128] = re_part.astype(BF16)
+            matrix[direction, :64, 128:] = (-im_part).astype(BF16)
+            matrix[direction, 64:, :128] = im_part.astype(BF16)
+            matrix[direction, 64:, 128:] = re_part.astype(BF16)
         rim_re, rim_im = real[:, 128:], imag[:, 128:]
         lane = lax.broadcasted_iota(jnp.int32, (128, 128), 1)
 
@@ -246,8 +288,11 @@
             high = jnp.where(lane < 96, pltpu.roll(second, 64, 1), second)
             return jnp.where(lane < 64, low, high)
 
-        row_halo[direction, :128, :] = weave(rim_re, -rim_im).astype(BF16)
-        row_halo[direction, 128:, :] = weave(rim_im, rim_re).astype(BF16)
+        def rim(part):
+            return jnp.concatenate([part[:HALF], part[ROWS - HALF :]], axis=0).astype(BF16)
+
+        row_halo[direction, :64, :] = rim(weave(rim_re, -rim_im))
+        row_halo[direction, 64:, :] = rim(weave(rim_im, rim_re))
         for part in range(2):
             factor = 1.0 if part == 0 else sign
             far_part = factor * toeplitz(turned + part, 96)[:, :128]
@@ -263,9 +308,33 @@
             low, high = max(0, j - 1), min(4, j + 2)
             weights = col_w[direction, (low - j + 1) * 128 : (high - j + 1) * 128, :]
             both = dot(field[:, low * 128 : high * 128], weights)
-            reals.append(both[:128, :128] - both[128:, 128:])
-            imags.append(both[:128, 128:] + both[128:, :128])
+            reals.append(both[:64, :128] - both[64:, 128:])
+            imags.append(both[:64, 128:] + both[64:, :128])
         return jnp.concatenate(reals, axis=1), jnp.concatenate(imags, axis=1)
+
+    top, middle, bottom = (
+        pl.ds(0, HALF),
+        pl.ds(HALF, ROWS - 2 * HALF),
+        pl.ds(ROWS - HALF, HALF),
+    )
+
+    def get_rim(ref):
+        return jnp.concatenate(
+            [ref[part, rows, :] for part in range(2) for rows in (top, bottom)], axis=0
+        )
+
+    def put_rim(ref, real, imag):
+        for part, value in ((0, real), (1, imag)):
+            value = value.astype(BF16)
+            ref[part, top, :] = value[:HALF]
+            ref[part, bottom, :] = value[HALF:]
+
+    def get_core(ref):
+        return jnp.concatenate([ref[0, middle, :], ref[1, middle, :]], axis=0)
+
+    def put_core(ref, real, imag):
+        ref[0, middle, :] = real.astype(BF16)
+        ref[1, middle, :] = imag.astype(BF16)
 
     def halo_copies(step, field):
         above = pltpu.make_async_remote_copy(
@@ -314,11 +383,14 @@
             else:
                 below.wait_recv()
 
-    def along_rows(step, field, direction):
-        acc[...] = dot(row_own[direction], field[...].reshape(2 * ROWS, WIN))
+    def core_rows(field, direction):
+        own = field[...].reshape(2 * ROWS, WIN)
+        acc[...] = dot(row_rim[direction], own)
+        return dot(row_core[direction], own)
+
+    def rim_rows(step, field, direction):
         halo_wait(step, field, False)
-        rim = halo[step].reshape(4 * HALF, WIN)
-        return acc[...] + dot(row_halo[direction], rim)
+        return acc[...] + dot(row_halo[direction], halo[step].reshape(4 * HALF, WIN))
 
     @pl.when(is_member)
     def _():
@@ -333,6 +405,12 @@
         ]
         for copy in tables:
             copy.start()
+        line[...] = jnp.zeros_like(line)
+        line[0:2, 0 : 2 * HALF + 1] = taps[...].astype(F32)
+        first = lax.broadcasted_iota(jnp.int32, (128, 128), 0)
+        second = lax.broadcasted_iota(jnp.int32, (128, 128), 1)
+        mirror = jnp.where(first + second == 2 * HALF, 1.0, 0.0).astype(BF16)
+        line[8:, :128] = dot(line[:8, :128].astype(BF16), mirror)
         build(0)
         build(1)
 
@@ -347,35 +425,59 @@
         for copy in tables:
             copy.wait()
 
-        def forward(s, _):
+        def arrived(s):
             for j in range(2):
                 part = trans.at[s, :, pl.ds(j * STRIP, STRIP), :]
                 pltpu.make_async_copy(part, part, win_recv.at[s, j]).wait()
-            field = lits.at[s]
-
-            def light(rows):
-                wave_re = waves[s, 0, rows, :].astype(F32)
-                wave_im = waves[s, 1, rows, :].astype(F32)
-                trans_re = trans[s, 0, rows, :].astype(F32)
-                trans_im = trans[s, 1, rows, :].astype(F32)
-                field[0, rows, :] = (wave_re * trans_re - wave_im * trans_im).astype(BF16)
-                field[1, rows, :] = (wave_re * trans_im + wave_im * trans_re).astype(BF16)
-
-            light(pl.ds(0, HALF))
-            light(pl.ds(ROWS - HALF, HALF))
-            halo_start(s, field)
-            light(pl.ds(HALF, ROWS - 2 * HALF))
-            mid = along_rows(s, field, 0).astype(BF16)
-            real, imag = along_columns(mid, 0)
-            waves[s + 1, 0] = real.astype(BF16)
-            waves[s + 1, 1] = imag.astype(BF16)
+
+        def light(s, wave, get, put):
+            wave_re, wave_im = wave
+            both = get(trans.at[s]).astype(F32)
+            trans_re, trans_im = both[:64], both[64:]
+            put(
+                lits.at[s],
+                wave_re * trans_re - wave_im * trans_im,
+                wave_re * trans_im + wave_im * trans_re,
+            )
+
+        def kept(s, get):
+            both = get(waves.at[s]).astype(F32)
+            return both[:64], both[64:]
+
+        arrived(0)
+        light(0, kept(0, get_rim), get_rim, put_rim)
+        halo_start(0, lits.at[0])
+
+        def forward(s, _):
+            @pl.when(s + AHEAD < SLICES)
+            def _():
+                ask(s + AHEAD)
+
+            light(s, kept(s, get_core), get_core, put_core)
+            mid = core_rows(lits.at[s], 0).astype(BF16)
+            put_core(waves.at[s + 1], *along_columns(mid, 0))
+
+            @pl.when(s < SLICES - 1)
+            def _():
+                arrived(s + 1)
+
+            mid = rim_rows(s, lits.at[s], 0).astype(BF16)
+            put_rim(waves.at[s + 1], *along_columns(mid, 0))
+
+            @pl.when(s < SLICES - 1)
+            def _():
+                light(s + 1, kept(s + 1, get_rim), get_rim, put_rim)
+                halo_start(s + 1, lits.at[s + 1])
+
             return 0
 
         lax.fori_loop(0, SLICES, forward, 0)
 
         for i in range(16):
             pltpu.make_async_copy(int_in.at[i], int_in.at[i], int_recv.at[i]).wait()
-        int_t[...] = int_in[...].reshape(128, WIN).T
+        for part in range(2):
+            values = int_in[:, part * 8 : part * 8 + 8, :].astype(F32).reshape(128, WIN // 2)
+            int_t[part * (WIN // 2) : (part + 1) * (WIN // 2), :] = values.T
 
         exit_wave = waves[SLICES].reshape(2 * ROWS, WIN)
         by_cos, by_sin = dot(exit_wave, cos_t[...]), dot(exit_wave, sin_t[...])
@@ -460,20 +562,7 @@
                 device_id_type=MESH,
             )
 
-        def backward(i, _):
-            s = SLICES - 1 - i
-            step = SLICES + s
-            field = gmids.at[s]
-            real, imag = along_columns(gwave[...].reshape(2 * ROWS, WIN), 1)
-            field[0] = real.astype(BF16)
-            field[1] = imag.astype(BF16)
-            halo_start(step, field)
-            glit = along_rows(step, field, 1)
-            glit_re, glit_im = glit[:128], glit[128:]
-            seen_re = waves[s, 0].astype(F32)
-            seen_im = waves[s, 1].astype(F32)
-            incs[s, 0] = (glit_re * seen_re + glit_im * seen_im).astype(BF16)
-            incs[s, 1] = (glit_im * seen_re - glit_re * seen_im).astype(BF16)
+        def inc_start(s):
             for j in range(2):
                 local = same(inc_target(s, j), me)
 
@@ -487,13 +576,54 @@
                 def _():
                     inc_copy(s, j).start()
 
-            trans_re = trans[s, 0].astype(F32)
-            trans_im = trans[s, 1].astype(F32)
-            gwave[0] = (trans_re * glit_re + trans_im * glit_im).astype(BF16)
-            gwave[1] = (trans_re * glit_im - trans_im * glit_re).astype(BF16)
+        def increment(s, glit, get, put):
+            seen_re, seen_im = kept(s, get)
+            glit_re, glit_im = glit[:64], glit[64:]
+            put(
+                incs.at[s],
+                glit_re * seen_re + glit_im * seen_im,
+                glit_im * seen_re - glit_re * seen_im,
+            )
+
+        def pull(s, glit, get, put):
+            both = get(trans.at[s]).astype(F32)
+            trans_re, trans_im = both[:64], both[64:]
+            glit_re, glit_im = glit[:64], glit[64:]
+            put(
+                gwave,
+                trans_re * glit_re + trans_im * glit_im,
+                trans_re * glit_im - trans_im * glit_re,
+            )
+
+        def send_rim(s):
+            put_rim(gmids.at[s], *along_columns(get_rim(gwave), 1))
+            halo_start(SLICES + s, gmids.at[s])
+
+        send_rim(SLICES - 1)
+
+        def backward(i, _):
+            s = SLICES - 1 - i
+
+            @pl.when(i > 0)
+            def _():
+                inc_start(s + 1)
+
+            put_core(gmids.at[s], *along_columns(get_core(gwave), 1))
+            glit = core_rows(gmids.at[s], 1)
+            increment(s, glit, get_core, put_core)
+            pull(s, glit, get_core, put_core)
+            glit = rim_rows(SLICES + s, gmids.at[s], 1)
+            pull(s, glit, get_rim, put_rim)
+
+            @pl.when(s > 0)
+            def _():
+                send_rim(s - 1)
+
+            increment(s, glit, get_rim, put_rim)
             return 0
 
         lax.fori_loop(0, SLICES, backward, 0)
+        inc_start(0)
 
         def settle(s, _):
             halo_wait(s, lits.at[s], True)
@@ -521,7 +651,7 @@
         pltpu.make_async_copy(out.at[p], out.at[p], inc_recv.at[p]).wait()
 
 
-def chain(win, ints, probe, line):
+def chain(win, ints, probe, taps):
     hbm = pl.BlockSpec(memory_space=pl.ANY)
     vmem = pl.BlockSpec(memory_space=pltpu.VMEM)
     cos_table, sin_table = (jnp.asarray(t, BF16) for t in fourier_tables())
@@ -533,25 +663,28 @@
         out_specs=hbm,
         out_shape=jax.ShapeDtypeStruct((4, 2, STRIP, WIN), BF16),
         scratch_shapes=[
+            pltpu.VMEM((16, 256), F32),
             pltpu.VMEM((SLICES,) + group, BF16),
             pltpu.VMEM((SLICES + 1,) + group, BF16),
             pltpu.VMEM((SLICES,) + group, BF16),
             pltpu.VMEM((SLICES,) + group, BF16),
             pltpu.VMEM((SLICES,) + group, BF16),
             pltpu.VMEM((2 * SLICES, 2, 2, HALF, WIN), BF16),
-            pltpu.VMEM((2 * ROWS, WIN), F32),
+            pltpu.VMEM((ROWS, WIN), F32),
             pltpu.VMEM(group, BF16),
-            pltpu.VMEM((2, 256, 256), BF16),
-            pltpu.VMEM((2, 256, 128), BF16),
+            pltpu.VMEM((2, 128, 256), BF16),
+            pltpu.VMEM((2, 128, 256), BF16),
+            pltpu.VMEM((2, 128, 128), BF16),
             pltpu.VMEM((2, 384, 256), BF16),
             pltpu.VMEM((WIN, WIN), BF16),
             pltpu.VMEM((WIN, WIN), BF16),
-            pltpu.VMEM((16, 8, WIN), F32),
+            pltpu.VMEM((16, 16, WIN // 2), BF16),
             pltpu.VMEM((WIN, 128), F32),
             pltpu.VMEM((4, 128, 256), BF16),
             pltpu.VMEM((WIN, 256), BF16),
             pltpu.VMEM((4, 128, 256), BF16),
             pltpu.VMEM((4, 128, 256), BF16),
+            pltpu.SemaphoreType.REGULAR,
             dma((4,)),
             dma((SLICES, 2)),
             dma((4,)),
@@ -567,10 +700,10 @@
             dma((3,)),
         ],
         compiler_params=pltpu.CompilerParams(
-            collective_id=0, has_side_effects=True, vmem_limit_bytes=48 << 20
+            collective_id=0, has_side_effects=True, vmem_limit_bytes=60 << 20
         ),
         name="chain",
-    )(win, ints, probe, line, cos_table, sin_table)
+    )(win, ints, probe, taps, cos_table, sin_table)
 
 
 def on_device(phase, absorption, probe, taps, offsets, intensity):
@@ -578,10 +711,8 @@
     band = ((lax.axis_index("tile") + 60) % 64) // 8
     starts = lax.dynamic_slice_in_dim(offsets, band * 2, 2, 1).reshape(4)
     info = jnp.concatenate([starts, slab[None].astype(jnp.int32)])
-    both = jnp.concatenate([taps, taps[:, ::-1]], axis=0).astype(F32)
-    line = jnp.pad(both, ((0, 4), (0, 256 - both.shape[1])))
     win, trans, ints = prepare(info, phase[0], absorption[0], intensity)
-    inc = chain(win, ints, probe, line)
+    inc = chain(win, ints, probe, taps)
     return finish(info, inc, trans)[None]
 
 

time: 123 us -> 114 us (0.927)
  Pallas kernels: 115 us -> 111 us
  local copies, waits for them, and re-layouts: 5.74 us -> 1.88 us
    pallas_call x1, Pallas kernels: 112 us -> 104 us  [chain(): pl.pallas_call(chain_kernel, in_specs=[hbm, hbm, hbm, vmem, hbm, hbm], ou...]
    pallas_call x1, Pallas kernels: 1.57 us -> 4.76 us  [prepare(): pl.pallas_call(prepare_kernel, grid_spec=pltpu.PrefetchScalarGridSpec(num...]
    unnamed x14 -> x8, local copies, waits for them, and re-layouts: 4.84 us -> 1.72 us
where the time goes in v2:
time: 114 us
  Pallas kernels  111 us (97%)
  local copies, waits for them, and re-layouts  1.88 us (2%)
    pallas_call x1, Pallas kernels, chain(): pl.pallas_call(chain_kernel, in_specs=[hbm, hbm, hbm, vmem, hbm, hbm], ou...  104 us
    pallas_call x1, Pallas kernels, prepare(): pl.pallas_call(prepare_kernel, grid_spec=pltpu.PrefetchScalarGridSpec(num...  4.76 us

profile of v2, /device:TPU:1, one launch (start us, length us, event | category | flops | bytes accessed | tf_op | source)
XLA Modules:
  0.0 113.6 jit_solution(18052955248622344786)
XLA Ops:
  0.0 0.0 copy-start
  0.0 0.7 copy-done
  0.7 0.1 constant_dynamic-slice_fusion
  0.8 0.1 reshape.3
  0.8 0.6 pad_add_fusion.info
  1.4 4.8 %prepare.1 = (bf16[4,2,64,512]{3,2,1,0:T(8,128)(2,1)}, f32[2,64,2048]{2,1,0:T(8,128)}, bf16[4,16,256]{2,1,0:T(8,128)(2,1)}) custom-call(s32[5]{0:T(128)} %pad_add_fusion.info, f32[64,2048]{1,0:T(8,128)} %bitcast.4, f32[64,2048]{1,0:T(8,128)} %bitcast.5, f32[2,8,8,2,512]{4,3,2,1,0:T(2,128)} %intensity.1), custom_call_target="tpu_custom_call" | custom-call | tf_op jit(solution)/shard_map/prepare/pallas_call | solution.py:77
  6.2 0.0 copy-start.2
  6.2 0.0 copy-start.3
  6.2 104.1 %chain.1.inc = bf16[4,2,64,512]{3,2,1,0:T(8,128)(2,1)} custom-call(bf16[4,2,64,512]{3,2,1,0:T(8,128)(2,1)} %get-tuple-element.8.win, bf16[4,16,256]{2,1,0:T(8,128)(2,1)} %get-tuple-element.9.ints, bf16[2,512,512]{2,1,0:T(8,128)(2,1)} %probe.1, bf16[2,65]{1,0:T(2,128)(2,1)} %taps.1, bf16[512,512]{1,0:T(8,128)(2,1)} %constant.48.clone.cos_hbm, ...), custom_call_target="tpu_custom_call" | custom-call | tf_op jit(solution)/shard_map/chain/pallas_call | solution.py:660
  110.3 0.0 copy-done.2
  110.3 0.0 copy-done.3
  110.3 0.0 copy-start.1
  110.3 1.0 copy-done.1
  111.4 2.3 %finish.1 = f32[2,64,2048]{2,1,0:T(8,128)} custom-call(s32[5]{0:T(128)S(1)} %copy-done.3, bf16[4,2,64,512]{3,2,1,0:T(8,128)(2,1)S(1)} %copy-done.1, f32[2,64,2048]{2,1,0:T(8,128)S(1)} %copy-done.2), custom_call_target="tpu_custom_call" | custom-call | tf_op jit(solution)/shard_map/finish/pallas_call | solution.py:121
Async XLA Ops:
  0.0 0.7 copy-start
  6.2 104.1 %copy-start.2 = (f32[2,64,2048]{2,1,0:T(8,128)S(1)}, f32[2,64,2048]{2,1,0:T(8,128)}, u32[]{:S(2)}) copy-start(f32[2,64,2048]{2,1,0:T(8,128)} %get-tuple-element.10.trans) | copy-start | bytes 3145732
  6.2 104.1 %copy-start.3 = (s32[5]{0:T(128)S(1)}, s32[5]{0:T(128)}, u32[]{:S(2)}) copy-start(s32[5]{0:T(128)} %pad_add_fusion.info) | copy-start | bytes 64
  110.3 1.0 copy-start.1

commit v3 on v2

--- a/solution.py
+++ b/solution.py
@@ -45,71 +45,21 @@
     return 2.0 * s * c, 1.0 - 2.0 * s * s
 
 
-CHUNK = 16
-
-
-def prepare_kernel(info, phase, absorb, intensity, win, trans, ints, wide):
-    sin_part, cos_part = sincos(phase[...])
-    decay = jnp.exp(-absorb[...])
-    real, imag = decay * cos_part, decay * sin_part
-    trans[0] = real
-    trans[1] = imag
-    wide[0, :, :NXO] = real
-    wide[1, :, :NXO] = imag
-    wide[:, :, NXO:] = jnp.zeros((2, CHUNK, 128), F32)
-    for p in range(4):
-        start = info[p]
-        base = pl.multiple_of(start // 128 * 128, 128)
-        turn = (640 - start % 128) % 640
-        for part in range(2):
-            block = wide[part, :, pl.ds(base, 640)]
-            win[p, part] = pltpu.roll(block, turn, 1)[:, :WIN].astype(BF16)
-
-    @pl.when(pl.program_id(0) == 0)
-    def _():
-        for p in range(4):
-            values = intensity[p // 2, :, 0, p % 2, :]
-            halves = [values[:, : WIN // 2], values[:, WIN // 2 :]]
-            ints[p] = jnp.concatenate(halves, axis=0).astype(BF16)
-
-
-def prepare(info, phase, absorb, intensity):
-    return pl.pallas_call(
-        prepare_kernel,
-        grid_spec=pltpu.PrefetchScalarGridSpec(
-            num_scalar_prefetch=1,
-            grid=(STRIP // CHUNK,),
-            in_specs=[
-                pl.BlockSpec((CHUNK, NXO), lambda i, info: (i, 0)),
-                pl.BlockSpec((CHUNK, NXO), lambda i, info: (i, 0)),
-                pl.BlockSpec((2, 8, 1, 2, WIN), lambda i, info: (0, 0, info[4], 0, 0)),
-            ],
-            out_specs=[
-                pl.BlockSpec((4, 2, CHUNK, WIN), lambda i, info: (0, 0, i, 0)),
-                pl.BlockSpec((2, CHUNK, NXO), lambda i, info: (0, i, 0)),
-                pl.BlockSpec((4, 16, WIN // 2), lambda i, info: (0, 0, 0)),
-            ],
-            scratch_shapes=[pltpu.VMEM((2, CHUNK, NXO + 128), F32)],
-        ),
-        out_shape=[
-            jax.ShapeDtypeStruct((4, 2, STRIP, WIN), BF16),
-            jax.ShapeDtypeStruct((2, STRIP, NXO), F32),
-            jax.ShapeDtypeStruct((4, 16, WIN // 2), BF16),
-        ],
-        compiler_params=pltpu.CompilerParams(vmem_limit_bytes=60 << 20),
-        name="prepare",
-    )(info, phase, absorb, intensity)
-
-
-def finish_kernel(info, inc, trans, out, wide):
+def finish_kernel(info, inc_hbm, trans_hbm, out, inc, trans, wide, sems):
+    copies = [pltpu.make_async_copy(inc_hbm.at[p], inc.at[p], sems.at[p]) for p in range(4)]
+    copies.append(pltpu.make_async_copy(trans_hbm, trans, sems.at[4]))
+    for copy in copies:
+        copy.start()
     wide[...] = jnp.zeros_like(wide)
     blank = jnp.zeros((STRIP, 128), F32)
     for p in range(4):
+        copies[p].wait()
         start = info[p]
         base = pl.multiple_of(start // 128 * 128, 128)
         for part in range(2):
             block = jnp.concatenate([inc[p, part].astype(F32), blank], axis=1)
             wide[part, :, pl.ds(base, 640)] += pltpu.roll(block, start % 128, 1)
+    copies[4].wait()
     real, imag = trans[0], trans[1]
     grad_re, grad_im = wide[0, :, :NXO], wide[1, :, :NXO]
     out[0] = grad_im * real - grad_re * imag
@@ -117,14 +67,20 @@
 
 
 def finish(info, inc, trans):
+    hbm = pl.BlockSpec(memory_space=pl.ANY)
     vmem = pl.BlockSpec(memory_space=pltpu.VMEM)
     return pl.pallas_call(
         finish_kernel,
-        in_specs=[pl.BlockSpec(memory_space=pltpu.SMEM), vmem, vmem],
+        in_specs=[pl.BlockSpec(memory_space=pltpu.SMEM), hbm, hbm],
         out_specs=vmem,
         out_shape=jax.ShapeDtypeStruct((2, STRIP, NXO), F32),
-        scratch_shapes=[pltpu.VMEM((2, STRIP, NXO + 128), F32)],
-        compiler_params=pltpu.CompilerParams(vmem_limit_bytes=32 << 20),
+        scratch_shapes=[
+            pltpu.VMEM((4, 2, STRIP, WIN), BF16),
+            pltpu.VMEM((2, STRIP, NXO), F32),
+            pltpu.VMEM((2, STRIP, NXO + 128), F32),
+            pltpu.SemaphoreType.DMA((5,)),
+        ],
+        compiler_params=pltpu.CompilerParams(vmem_limit_bytes=60 << 20),
         name="finish",
     )(info, inc, trans)
 
@@ -147,12 +103,12 @@
 
 
 def chain_kernel(
-    win, ints, probe, taps, cos_hbm, sin_hbm, out,
-    line, trans, waves, lits, gmids, incs, halo, acc, gwave,
+    info, phase_hbm, absorb_hbm, intensity_hbm, probe, taps, cos_hbm, sin_hbm, out, full_out,
+    phase, absorb, intensity, full, win, ints, line, trans, waves, lits, gmids, incs, halo, acc, gwave,
     row_rim, row_core, row_halo, col_w, cos_t, sin_t, int_in, int_t,
     stage, spec_in, back_out, back_in,
     credit, win_send, win_recv, int_send, int_recv, halo_send, halo_recv,
-    inc_send, inc_recv, spec_send, spec_recv, back_send, back_recv, table_sem,
+    inc_send, inc_recv, spec_send, spec_recv, back_send, back_recv, table_sem, load_sem,
 ):
     slab = lax.axis_index("slab")
     tile = lax.axis_index("tile")
@@ -165,6 +121,14 @@
     p_me = x
     c_me = upper * 2 + (tile % 2 + upper) % 2
 
+    loads = [
+        pltpu.make_async_copy(phase_hbm, phase, load_sem.at[0]),
+        pltpu.make_async_copy(absorb_hbm, absorb, load_sem.at[1]),
+        pltpu.make_async_copy(intensity_hbm.at[:, :, slab], intensity, load_sem.at[2]),
+    ]
+    for copy in loads:
+        copy.start()
+
     def signal(device):
         pl.semaphore_signal(pltpu.get_barrier_semaphore(), 1, device_id=device, device_id_type=MESH)
 
@@ -181,6 +145,32 @@
 
     for p in range(4):
         signal(member_at(band, jnp.int32(p), w // 2))
+
+    for copy in loads:
+        copy.wait()
+    for part in range(4):
+        rows = pl.ds(part * 16, 16)
+        sin_part, cos_part = sincos(phase[rows, :])
+        decay = jnp.exp(-absorb[rows, :])
+        full[0, rows, :NXO] = decay * cos_part
+        full[1, rows, :NXO] = decay * sin_part
+    full[:, :, NXO:] = jnp.zeros((2, STRIP, 512), F32)
+    for p in range(4):
+        start = info[p]
+        for part in range(2):
+            block = full[part]
+            for step, width in ((1024, 1536), (512, 1024), (256, 768), (128, 640)):
+                shifted = jnp.full((STRIP, width), start) & step
+                block = jnp.where(shifted > 0, block[:, step : step + width], block[:, :width])
+            for step in (64, 32, 16, 8, 4, 2, 1):
+                shifted = jnp.full((STRIP, 640), start) & step
+                block = jnp.where(shifted > 0, pltpu.roll(block, 640 - step, 1), block)
+            win[p, part] = block[:, :WIN].astype(BF16)
+        values = intensity[p // 2, :, p % 2, :]
+        halves = [values[:, : WIN // 2], values[:, WIN // 2 :]]
+        ints[p] = jnp.concatenate(halves, axis=0).astype(BF16)
+    full_copy = pltpu.make_async_copy(full.at[:, :, :NXO], full_out, load_sem.at[3])
+    full_copy.start()
     barrier = pltpu.get_barrier_semaphore()
 
     @pl.when(is_member)
@@ -649,9 +639,10 @@
             pltpu.make_async_copy(ints.at[p], ints.at[p], int_send.at[p]).wait()
 
         pltpu.make_async_copy(out.at[p], out.at[p], inc_recv.at[p]).wait()
-
-
-def chain(win, ints, probe, taps):
+    full_copy.wait()
+
+
+def chain(info, phase, absorb, intensity, probe, taps):
     hbm = pl.BlockSpec(memory_space=pl.ANY)
     vmem = pl.BlockSpec(memory_space=pltpu.VMEM)
     cos_table, sin_table = (jnp.asarray(t, BF16) for t in fourier_tables())
@@ -659,10 +650,19 @@
     group = (2, ROWS, WIN)
     return pl.pallas_call(
         chain_kernel,
-        in_specs=[hbm, hbm, hbm, vmem, hbm, hbm],
-        out_specs=hbm,
-        out_shape=jax.ShapeDtypeStruct((4, 2, STRIP, WIN), BF16),
+        in_specs=[pl.BlockSpec(memory_space=pltpu.SMEM), hbm, hbm, hbm, hbm, vmem, hbm, hbm],
+        out_specs=[hbm, hbm],
+        out_shape=[
+            jax.ShapeDtypeStruct((4, 2, STRIP, WIN), BF16),
+            jax.ShapeDtypeStruct((2, STRIP, NXO), F32),
+        ],
         scratch_shapes=[
+            pltpu.VMEM((STRIP, NXO), F32),
+            pltpu.VMEM((STRIP, NXO), F32),
+            pltpu.VMEM((2, 8, 2, WIN), F32),
+            pltpu.VMEM((2, STRIP, NXO + 512), F32),
+            pltpu.VMEM((4, 2, STRIP, WIN), BF16),
+            pltpu.VMEM((4, 16, WIN // 2), BF16),
             pltpu.VMEM((16, 256), F32),
             pltpu.VMEM((SLICES,) + group, BF16),
             pltpu.VMEM((SLICES + 1,) + group, BF16),
@@ -698,21 +698,19 @@
             dma((4,)),
             dma((4,)),
             dma((3,)),
+            dma((4,)),
         ],
         compiler_params=pltpu.CompilerParams(
             collective_id=0, has_side_effects=True, vmem_limit_bytes=60 << 20
         ),
         name="chain",
-    )(win, ints, probe, taps, cos_table, sin_table)
+    )(info, phase, absorb, intensity, probe, taps, cos_table, sin_table)
 
 
 def on_device(phase, absorption, probe, taps, offsets, intensity):
-    slab = lax.axis_index("slab")
     band = ((lax.axis_index("tile") + 60) % 64) // 8
-    starts = lax.dynamic_slice_in_dim(offsets, band * 2, 2, 1).reshape(4)
-    info = jnp.concatenate([starts, slab[None].astype(jnp.int32)])
-    win, trans, ints = prepare(info, phase[0], absorption[0], intensity)
-    inc = chain(win, ints, probe, taps)
+    info = lax.dynamic_slice_in_dim(offsets, band * 2, 2, 1).reshape(4)
+    inc, trans = chain(info, phase[0], absorption[0], intensity, probe, taps)
     return finish(info, inc, trans)[None]
 
 

time: 114 us -> 112 us (0.982)
    pallas_call x2 -> x1, Pallas kernels: 109 us -> 107 us  [chain(): pl.pallas_call(chain_kernel, in_specs=[pl.BlockSpec(memory_space=pltpu.SM...]
where the time goes in v3:
time: 112 us; the launch traced here: 111 us
  Pallas kernels  110 us (98%)
  local copies, waits for them, and re-layouts  1.37 us (1%)
    pallas_call x1, Pallas kernels, chain(): pl.pallas_call(chain_kernel, in_specs=[pl.BlockSpec(memory_space=pltpu.SM...  107 us
    pallas_call x1, Pallas kernels, finish(): pl.pallas_call(finish_kernel, in_specs=[pl.BlockSpec(memory_space=pltpu.S...  3.38 us

profile of v3, /device:TPU:1, one launch (start us, length us, event | category | flops | bytes accessed | tf_op | source)
XLA Modules:
  0.0 111.5 jit_solution(1843059334720241718)
XLA Ops:
  0.0 0.0 copy-start
  0.0 0.7 copy-done
  0.7 0.1 constant_dynamic-slice_fusion
  0.8 0.6 reshape.3.info
  1.4 106.7 %chain.1 = (bf16[4,2,64,512]{3,2,1,0:T(8,128)(2,1)}, f32[2,64,2048]{2,1,0:T(8,128)}) custom-call(s32[4]{0:T(128)} %reshape.3.info, f32[64,2048]{1,0:T(8,128)} %bitcast.3, f32[64,2048]{1,0:T(8,128)} %bitcast.4, f32[2,8,8,2,512]{4,3,2,1,0:T(2,128)} %intensity_hbm.1, bf16[2,512,512]{2,1,0:T(8,128)(2,1)} %probe.1, bf16[2,65]{1,0:T(2,128)(2,1)} %taps.1, ...), custom_call_target="tpu_custom_call" | custom-call | tf_op jit(solution)/shard_map/chain/pallas_call | solution.py:651
  108.1 3.4 %finish.1 = f32[2,64,2048]{2,1,0:T(8,128)} custom-call(s32[4]{0:T(128)} %reshape.3.info, bf16[4,2,64,512]{3,2,1,0:T(8,128)(2,1)} %get-tuple-element.7.inc_hbm, f32[2,64,2048]{2,1,0:T(8,128)} %get-tuple-element.8.trans_hbm), custom_call_target="tpu_custom_call" | custom-call | tf_op jit(solution)/shard_map/finish/pallas_call | solution.py:72
Async XLA Ops:
  0.0 0.7 copy-start

commit v4 on v3

--- a/solution.py
+++ b/solution.py
@@ -157,15 +157,23 @@
     full[:, :, NXO:] = jnp.zeros((2, STRIP, 512), F32)
     for p in range(4):
         start = info[p]
+        blocks = []
         for part in range(2):
             block = full[part]
             for step, width in ((1024, 1536), (512, 1024), (256, 768), (128, 640)):
                 shifted = jnp.full((STRIP, width), start) & step
                 block = jnp.where(shifted > 0, block[:, step : step + width], block[:, :width])
-            for step in (64, 32, 16, 8, 4, 2, 1):
-                shifted = jnp.full((STRIP, 640), start) & step
-                block = jnp.where(shifted > 0, pltpu.roll(block, 640 - step, 1), block)
-            win[p, part] = block[:, :WIN].astype(BF16)
+            blocks.append(block.astype(BF16))
+        source = lax.broadcasted_iota(jnp.int32, (256, 128), 0)
+        place = lax.broadcasted_iota(jnp.int32, (256, 128), 1)
+        pick = jnp.where(source - place == (jnp.full((256, 128), start) & 127), 1.0, 0.0)
+        both = jnp.concatenate(blocks, axis=0)
+        tall = jnp.concatenate([both[:, j * 128 : j * 128 + 256] for j in range(4)], axis=0)
+        cut = dot(tall, pick.astype(BF16)).astype(BF16)
+        for j in range(4):
+            for part in range(2):
+                first = j * 128 + part * STRIP
+                win[p, part, :, j * 128 : (j + 1) * 128] = cut[first : first + STRIP]
         values = intensity[p // 2, :, p % 2, :]
         halves = [values[:, : WIN // 2], values[:, WIN // 2 :]]
         ints[p] = jnp.concatenate(halves, axis=0).astype(BF16)

time: 112 us -> 109 us (0.973)
  Pallas kernels: 110 us -> 107 us
    pallas_call x1, Pallas kernels: 107 us -> 104 us  [chain(): pl.pallas_call(chain_kernel, in_specs=[pl.BlockSpec(memory_space=pltpu.SM...]
where the time goes in v4:
time: 109 us
  Pallas kernels  107 us (98%)
  local copies, waits for them, and re-layouts  1.37 us (1%)
    pallas_call x1, Pallas kernels, chain(): pl.pallas_call(chain_kernel, in_specs=[pl.BlockSpec(memory_space=pltpu.SM...  104 us
    pallas_call x1, Pallas kernels, finish(): pl.pallas_call(finish_kernel, in_specs=[pl.BlockSpec(memory_space=pltpu.S...  3.38 us

profile of v4, /device:TPU:1, one launch (start us, length us, event | category | flops | bytes accessed | tf_op | source)
XLA Modules:
  0.0 108.8 jit_solution(8121938490670140020)
XLA Ops:
  0.0 0.0 copy-start
  0.0 0.7 copy-done
  0.7 0.1 constant_dynamic-slice_fusion
  0.8 0.6 reshape.3.info
  1.4 104.1 %chain.1 = (bf16[4,2,64,512]{3,2,1,0:T(8,128)(2,1)}, f32[2,64,2048]{2,1,0:T(8,128)}) custom-call(s32[4]{0:T(128)} %reshape.3.info, f32[64,2048]{1,0:T(8,128)} %bitcast.3, f32[64,2048]{1,0:T(8,128)} %bitcast.4, f32[2,8,8,2,512]{4,3,2,1,0:T(2,128)} %intensity_hbm.1, bf16[2,512,512]{2,1,0:T(8,128)(2,1)} %probe.1, bf16[2,65]{1,0:T(2,128)(2,1)} %taps.1, ...), custom_call_target="tpu_custom_call" | custom-call | tf_op jit(solution)/shard_map/chain/pallas_call | solution.py:659
  105.5 3.4 %finish.1 = f32[2,64,2048]{2,1,0:T(8,128)} custom-call(s32[4]{0:T(128)} %reshape.3.info, bf16[4,2,64,512]{3,2,1,0:T(8,128)(2,1)} %get-tuple-element.7.inc_hbm, f32[2,64,2048]{2,1,0:T(8,128)} %get-tuple-element.8.trans_hbm), custom_call_target="tpu_custom_call" | custom-call | tf_op jit(solution)/shard_map/finish/pallas_call | solution.py:72
Async XLA Ops:
  0.0 0.7 copy-start

commit v5 on v4

--- a/solution.py
+++ b/solution.py
@@ -460,13 +460,14 @@
                 arrived(s + 1)
 
             mid = rim_rows(s, lits.at[s], 0).astype(BF16)
-            put_rim(waves.at[s + 1], *along_columns(mid, 0))
+            real, imag = (value.astype(BF16) for value in along_columns(mid, 0))
 
             @pl.when(s < SLICES - 1)
             def _():
-                light(s + 1, kept(s + 1, get_rim), get_rim, put_rim)
+                light(s + 1, (real.astype(F32), imag.astype(F32)), get_rim, put_rim)
                 halo_start(s + 1, lits.at[s + 1])
 
+            put_rim(waves.at[s + 1], real, imag)
             return 0
 
         lax.fori_loop(0, SLICES, forward, 0)

time: 109 us -> 109 us (level)
  no operation moved by 1% of the time
where the time goes in v5:
time: 109 us
  Pallas kernels  107 us (98%)
  local copies, waits for them, and re-layouts  1.37 us (1%)
    pallas_call x1, Pallas kernels, chain(): pl.pallas_call(chain_kernel, in_specs=[pl.BlockSpec(memory_space=pltpu.SM...  104 us
    pallas_call x1, Pallas kernels, finish(): pl.pallas_call(finish_kernel, in_specs=[pl.BlockSpec(memory_space=pltpu.S...  3.38 us

profile of v5, /device:TPU:1, one launch (start us, length us, event | category | flops | bytes accessed | tf_op | source)
XLA Modules:
  0.0 108.9 jit_solution(16018550106011896865)
XLA Ops:
  0.0 0.0 copy-start
  0.0 0.7 copy-done
  0.7 0.1 constant_dynamic-slice_fusion
  0.8 0.6 reshape.3.info
  1.4 104.1 %chain.1 = (bf16[4,2,64,512]{3,2,1,0:T(8,128)(2,1)}, f32[2,64,2048]{2,1,0:T(8,128)}) custom-call(s32[4]{0:T(128)} %reshape.3.info, f32[64,2048]{1,0:T(8,128)} %bitcast.3, f32[64,2048]{1,0:T(8,128)} %bitcast.4, f32[2,8,8,2,512]{4,3,2,1,0:T(2,128)} %intensity_hbm.1, bf16[2,512,512]{2,1,0:T(8,128)(2,1)} %probe.1, bf16[2,65]{1,0:T(2,128)(2,1)} %taps.1, ...), custom_call_target="tpu_custom_call" | custom-call | tf_op jit(solution)/shard_map/chain/pallas_call | solution.py:660
  105.5 3.4 %finish.1 = f32[2,64,2048]{2,1,0:T(8,128)} custom-call(s32[4]{0:T(128)} %reshape.3.info, bf16[4,2,64,512]{3,2,1,0:T(8,128)(2,1)} %get-tuple-element.7.inc_hbm, f32[2,64,2048]{2,1,0:T(8,128)} %get-tuple-element.8.trans_hbm), custom_call_target="tpu_custom_call" | custom-call | tf_op jit(solution)/shard_map/finish/pallas_call | solution.py:72
Async XLA Ops:
  0.0 0.7 copy-start
